TPU v7x, 128 devices: a whole 4x4x4 slice. The times are simulated.
128 devices in a mesh: dp: 8 (over z, core), tensor: 16 (over x, y).
Axes of the slice: x: 4, y: 4, z: 4, core: 2. Of those that a mesh axis runs over, the one named last changes fastest.
Arguments:
- pool: bfloat16 [2048, 16, 64, 2, 128], P('dp', 'tensor'), may hold values from -12 to 12
- fresh_kv: bfloat16 [768, 16, 64, 2, 128], P(('dp', 'tensor')), may hold values from -12 to 12
- routes: int32 [768], replicated, may hold values from 0 to 7, as said below
- landing_order: int32 [8, 256], P('dp'), may hold values from 0 to 255, each once within a row
- pool_order: int32 [8, 256], P('dp'), may hold values from 0 to 255, each once within a row
- block_counts: int32 [8, 4], P('dp'), may hold values from 1 to 192, 256 in all within a row
- tail_fill: int32 [32], P('dp'), may hold values from 1 to 128
- queries: bfloat16 [32, 8192], P('dp', 'tensor'), may hold values from -200 to 200
- new_kv: bfloat16 [32, 8, 2, 128], P('dp'), may hold values from -12 to 12
- w_out: bfloat16 [8192, 8192], P('tensor'), may hold values from -0.0625 to 0.0625
- residual: bfloat16 [32, 8192], P('dp'), may hold values from -2 to 2
- gain: float32 [8192], replicated, may hold values from 0.5 to 1.5
Outputs:
- normed: bfloat16 [32, 8192], P('dp', 'tensor')
Inputs may be any that keep to these rules, and one draw needn't show every extreme that they name: `routes`: of the 6 blocks of one device at most 2 go to one group, and exactly 2 to some group.
All inputs are finite; a program needn't handle non-finite values.
Results may differ from a plain program's by a relative error of at most 0.0047.
Values may be sent and summed in bfloat16 or wider, within the bound.
A program may use at most 128 MiB of HBM per device.

v0:
```python
import math

import jax
import jax.numpy as jnp
from jax import lax
from jax.sharding import PartitionSpec as P

BLOCK_TOKENS = 128
CAPACITY = 2


def partner(block, axis, apart):
    count = lax.axis_size(axis)
    route = []
    for low in range(count):
        high = low | 1 << apart
        if high != low and high < count:
            route += [(low, high), (high, low)]
    return lax.ppermute(block, axis, route)


def block_scores(blocks, owners, live, all_heads, row_count, score_scale):
    block_count = blocks.shape[0]
    half_tokens = blocks.shape[1] // 2
    member = owners[None, :] == jnp.arange(row_count, dtype=jnp.int32)[:, None]
    slot_query = jnp.einsum(
        "rp,rgd->pgd", member.astype(jnp.bfloat16), all_heads, preferred_element_type=jnp.float32
    ).astype(jnp.bfloat16)
    both = (
        jnp.einsum("pgd,psd->pgs", slot_query, blocks, preferred_element_type=jnp.float32)
        * score_scale
    )
    scores = both.reshape(block_count, both.shape[1], half_tokens, 2)[..., 0]
    masked = jnp.where(live[:, None, :], scores, -jnp.inf)
    slot_max = jnp.max(masked, axis=-1)
    row_max = jnp.max(jnp.where(member[:, :, None], slot_max[None], -jnp.inf), axis=1)
    return (scores, member, row_max)


def block_sums(blocks, scores, member, live, row_top):
    block_count = blocks.shape[0]
    top_of = jnp.sum(jnp.where(member[:, :, None], row_top[:, None, :], 0.0), axis=0)
    weights = jnp.where(live[:, None, :], jnp.exp(scores - top_of[:, :, None]), 0.0)
    member_f = member.astype(jnp.float32)
    totals = jnp.einsum(
        "rp,pg->rg", member_f, jnp.sum(weights, axis=-1), precision=lax.Precision.HIGHEST
    )
    rounded = weights.astype(jnp.bfloat16)
    spaced = jnp.stack([jnp.zeros_like(rounded), rounded], axis=-1).reshape(
        block_count, rounded.shape[1], blocks.shape[1]
    )
    weighted = jnp.einsum("pgs,psd->pgd", spaced, blocks, preferred_element_type=jnp.float32)
    sums = jnp.einsum("rp,pgd->rgd", member_f, weighted, precision=lax.Precision.HIGHEST)
    return (totals, sums)


def local(
    pool,
    fresh_kv,
    routes,
    landing_order,
    pool_order,
    block_counts,
    tail_fill,
    queries,
    new_kv,
    w_out,
    residual,
    gain,
):
    dp_count = lax.axis_size("dp")
    tp_count = lax.axis_size("tensor")
    dp_place = lax.axis_index("dp")
    tp_place = lax.axis_index("tensor")
    sender = dp_place * tp_count + tp_place
    outgoing = fresh_kv.shape[0]
    pieces = fresh_kv.shape[1]
    half_tokens = fresh_kv.shape[2]
    head_dim = fresh_kv.shape[4]
    piece_size = half_tokens * 2 * head_dim
    pool_count = pool.shape[0]
    my_routes = lax.dynamic_slice_in_dim(routes, sender * outgoing, outgoing)
    order_ids = jnp.arange(outgoing, dtype=jnp.int32)
    earlier = (my_routes[:, None] == my_routes[None, :]) & (order_ids[None, :] < order_ids[:, None])
    my_ranks = jnp.sum(earlier.astype(jnp.int32), axis=1)
    targets = my_routes * CAPACITY + my_ranks
    picker = (jnp.arange(dp_count * CAPACITY, dtype=jnp.int32)[:, None] == targets[None, :]).astype(
        jnp.bfloat16
    )
    picker = picker.reshape(dp_count, CAPACITY, outgoing)
    flat_blocks = fresh_kv.reshape(outgoing, pieces, piece_size)
    every_route = routes.reshape(dp_count * tp_count, outgoing)
    sent_here = jnp.sum((every_route == dp_place).astype(jnp.int32), axis=1)
    sectioning = jnp.einsum(
        "dcf,ftr->dtcr", picker, flat_blocks, preferred_element_type=jnp.float32
    ).astype(jnp.bfloat16)
    sectioning = sectioning.reshape(dp_count * tp_count, CAPACITY, piece_size)
    received = lax.all_to_all(sectioning, ("dp", "tensor"), split_axis=0, concat_axis=0, tiled=True)
    source_ids = jnp.arange(dp_count * tp_count, dtype=jnp.int32)[:, None]
    slot_ids = jnp.arange(CAPACITY, dtype=jnp.int32)[None, :]
    grid_shape = received.shape[:-1]
    arrival_blocks = received.reshape(-1, 2 * half_tokens, head_dim)
    source_grid = jnp.broadcast_to(source_ids, grid_shape).reshape(-1)
    slot_grid = jnp.broadcast_to(slot_ids, grid_shape).reshape(-1)
    source_match = source_grid[:, None] == jnp.arange(dp_count * tp_count, dtype=jnp.int32)[None, :]
    sent_count = jnp.sum(jnp.where(source_match, sent_here[None, :], 0), axis=1)
    arrived_live = slot_grid < sent_count
    land_at = jnp.take(landing_order[0], source_grid * CAPACITY + slot_grid)
    land_at = jnp.where(arrived_live, land_at, pool_count)
    replaced = jnp.zeros((pool_count,), jnp.int32).at[land_at].set(1, mode="drop")
    resident = pool.reshape(pool_count, 2 * half_tokens, head_dim)
    order_here = pool_order[0]
    position_of = (
        jnp.zeros((pool_count,), jnp.int32)
        .at[order_here]
        .set(jnp.arange(pool_count, dtype=jnp.int32))
    )
    counts = block_counts[0]
    row_count = counts.shape[0]
    row_ends = jnp.cumsum(counts)
    starts = row_ends - counts
    owner_rows = jnp.sum((position_of[:, None] >= row_ends[None, :]).astype(jnp.int32), axis=1)
    member = owner_rows[None, :] == jnp.arange(row_count, dtype=jnp.int32)[:, None]
    starts_of = jnp.sum(jnp.where(member, starts[:, None], 0), axis=0)
    lengths = (counts - 1) * BLOCK_TOKENS + tail_fill
    length_of = jnp.sum(jnp.where(member, lengths[:, None], 0), axis=0)
    index_in_row = position_of - starts_of
    pair_half = tp_place % 2
    token_pos = (
        index_in_row[:, None] * BLOCK_TOKENS
        + pair_half * half_tokens
        + jnp.arange(half_tokens, dtype=jnp.int32)[None, :]
    )
    counted = token_pos < length_of[:, None]
    pool_live = counted & (replaced[:, None] == 0)
    safe_land = jnp.minimum(land_at, pool_count - 1)
    arrival_owner = jnp.take(owner_rows, safe_land)
    arrival_live = jnp.take(counted, safe_land, axis=0) & arrived_live[:, None]
    own_heads = queries.reshape(row_count, -1, head_dim)
    partner_heads = partner(queries, "tensor", 0).reshape(row_count, -1, head_dim)
    first_four = jnp.where(pair_half == 0, own_heads, partner_heads)
    second_four = jnp.where(pair_half == 0, partner_heads, own_heads)
    all_heads = jnp.concatenate([first_four, second_four], axis=1)
    kv_index = tp_place // 2
    token_new = lax.dynamic_index_in_dim(new_kv, kv_index, 1, keepdims=False)
    score_scale = 1.0 / math.sqrt(head_dim)
    pool_scores, pool_member, pool_max = block_scores(
        resident, owner_rows, pool_live, all_heads, row_count, score_scale
    )
    come_scores, come_member, come_max = block_scores(
        arrival_blocks, arrival_owner, arrival_live, all_heads, row_count, score_scale
    )
    new_score = (
        jnp.einsum("rgd,rd->rg", all_heads, token_new[:, 0, :], preferred_element_type=jnp.float32)
        * score_scale
    )
    local_top = jnp.maximum(jnp.maximum(pool_max, come_max), new_score)
    row_top = jnp.maximum(local_top, partner(local_top, "tensor", 0))
    pool_totals, pool_sums = block_sums(resident, pool_scores, pool_member, pool_live, row_top)
    come_totals, come_sums = block_sums(
        arrival_blocks, come_scores, come_member, arrival_live, row_top
    )
    totals = pool_totals + come_totals
    sums = pool_sums + come_sums
    new_weight = jnp.exp(new_score - row_top)
    first_half = (pair_half == 0).astype(jnp.float32)
    totals = totals + first_half * new_weight
    sums = sums + first_half * new_weight[..., None] * token_new[:, None, 1, :].astype(jnp.float32)
    quarter = all_heads.shape[1] // 2
    mine_start = pair_half * quarter
    other_start = (1 - pair_half) * quarter
    keep_sums = lax.dynamic_slice_in_dim(sums, mine_start, quarter, 1)
    keep_totals = lax.dynamic_slice_in_dim(totals, mine_start, quarter, 1)
    give_sums = lax.dynamic_slice_in_dim(sums, other_start, quarter, 1)
    give_totals = lax.dynamic_slice_in_dim(totals, other_start, quarter, 1)
    got_sums, got_totals = partner((give_sums, give_totals), "tensor", 0)
    attended = ((keep_sums + got_sums) / (keep_totals + got_totals)[..., None]).astype(jnp.bfloat16)
    attended = attended.reshape(row_count, quarter * head_dim)
    partial_sum = jnp.dot(attended, w_out, preferred_element_type=jnp.float32)
    full_width = w_out.shape[1]
    column_share = full_width // tp_count
    projected = lax.psum(partial_sum, "tensor")
    hidden = residual.astype(jnp.float32) + projected
    mean_square = jnp.mean(hidden * hidden, axis=-1, keepdims=True)
    normed_rows = hidden * lax.rsqrt(mean_square + 1e-05) * gain
    return lax.dynamic_slice_in_dim(normed_rows, tp_place * column_share, column_share, 1).astype(
        jnp.bfloat16
    )


def solution(mesh):
    return jax.shard_map(
        local,
        mesh=mesh,
        in_specs=(
            P("dp", "tensor", None, None, None),
            P(("dp", "tensor"), None, None, None, None),
            P(),
            P("dp", None),
            P("dp", None),
            P("dp", None),
            P("dp"),
            P("dp", "tensor"),
            P("dp", None, None, None),
            P("tensor", None),
            P("dp", None),
            P(),
        ),
        out_specs=P("dp", "tensor"),
        check_vma=False,
    )
```

profile of v0, /device:TPU:0, one launch (start us, length us, event | category | flops | bytes accessed | tf_op | source)
XLA Modules:
  0.0 310.0 jit_solution(11408841308916096326)
XLA Ops:
  6.5 4.8 %reshape.269 = bf16[6,16,16384]{2,1,0:T(8,128)(2,1)S(1)} reshape(bf16[6,16,64,2,128]{4,3,2,1,0:T(2,128)(2,1)} %param.15) | data formatting | bytes 6291456 | tf_op jit(solution)/shard_map/reshape | solution.py:91
  13.0 7.1 %fusion = bf16[8,16,2,16384]{3,0,1,2:T(8,128)(2,1)} fusion(bf16[6,16,16384]{2,1,0:T(8,128)(2,1)S(1)} %reshape.269, s32[6]{0:T(128)S(1)} %multiply_add_fusion.2, s32[8,2]{0,1:T(2,128)S(1)} %multiply_add_fusion), kind=kOutput, calls=%fused_computation.6 | convolution fusion | flops 54526048 | bytes 11534424 | tf_op jit(solution)/shard_map/dcf,ftr->dtcr/dot_general | solution.py:94
  20.2 11.2 %copy.94 = bf16[8,16,2,16384]{3,1,0,2:T(8,128)(2,1)} copy(bf16[8,16,2,16384]{3,0,1,2:T(8,128)(2,1)} %fusion) | data formatting | bytes 16777216 | tf_op jit(solution)/shard_map/convert_element_type | solution.py:96
  31.4 16.3 %copy.95 = bf16[128,2,16384]{2,1,0:T(2,128)(2,1)} copy(bf16[128,2,16384]{2,0,1:T(8,128)(2,1)} %bitcast.89) | data formatting | bytes 16777216 | tf_op jit(solution)/shard_map/reshape | solution.py:97
  47.7 11.7 %all-to-all-start = ((bf16[128,2,16384]{2,1,0:T(2,128)(2,1)}), bf16[128,2,16384]{2,1,0:T(2,128)(2,1)}, u32[]{:S(2)}, u32[]{:S(2)}) async-start(bf16[128,2,16384]{2,1,0:T(2,128)(2,1)} %copy.95), calls=%async_computation | async-start | bytes 16777216 | tf_op jit(solution)/shard_map/all_to_all | solution.py:98
  59.5 1.1 collective-permute-start
  61.4 1.4 scatter_custom_fusion
  62.9 1.9 gather_fusion.1
  65.1 1.9 gather_fusion.2
  67.1 1.4 scatter_custom_fusion.1
  69.8 85.1 %collective-permute-done = bf16[4,512]{1,0:T(4,128)(2,1)S(1)} collective-permute-done((bf16[4,512]{1,0:T(4,128)(2,1)S(1)}, bf16[4,512]{1,0:T(4,128)(2,1)S(1)}, u32[]{:S(2)}, u32[]{:S(2)}) %collective-permute-start) | collective-permute-done | bytes 4128 | tf_op jit(solution)/shard_map/ppermute | solution.py:19
  155.3 6.7 %convolution_multiply_fusion.1 = f32[256,8,128]{2,1,0:T(8,128)S(1)} fusion(bf16[256,128,128]{2,1,0:T(8,128)(2,1)} %bitcast.87, bf16[256,8,128]{2,0,1:T(8,128)(2,1)S(1)} %convolution_convert_fusion.2), kind=kOutput, calls=%fused_computation.10 | convolution fusion | flops 67371008 | bytes 9961472 | tf_op jit(solution)/shard_map/pgd,psd->pgs/dot_general | solution.py:30
  163.4 14.5 %reshape.271 = bf16[256,128,128]{2,1,0:T(8,128)(2,1)} reshape(bf16[128,2,16384]{2,1,0:T(2,128)(2,1)} %all-to-all-done) | data formatting | bytes 16777216 | tf_op jit(solution)/shard_map/reshape | solution.py:102
  177.9 6.7 %convolution_multiply_fusion = f32[256,8,128]{2,1,0:T(8,128)S(1)} fusion(bf16[256,128,128]{2,1,0:T(8,128)(2,1)} %reshape.271, bf16[256,8,128]{2,0,1:T(8,128)(2,1)S(1)} %convolution_convert_fusion.1), kind=kOutput, calls=%fused_computation.9 | convolution fusion | flops 67371008 | bytes 9961472 | tf_op jit(solution)/shard_map/pgd,psd->pgs/dot_general | solution.py:30
  184.6 1.6 copy.97
  187.9 3.6 %collective-permute-done.1 = f32[4,8]{1,0:T(4,128)S(1)} collective-permute-done((f32[4,8]{1,0:T(4,128)S(1)}, f32[4,8]{1,0:T(4,128)S(1)}, u32[]{:S(2)}, u32[]{:S(2)}) %collective-permute-start.1) | collective-permute-done | bytes 160 | tf_op jit(solution)/shard_map/ppermute | solution.py:19
  191.9 1.2 select_convert_fusion
  194.0 4.7 %fusion.44 = f32[256,8,128]{2,1,0:T(8,128)S(1)} fusion(bf16[256,8,128]{2,1,0:T(8,128)(2,1)S(1)} %copy.99, bf16[256,128,128]{2,1,0:T(8,128)(2,1)} %bitcast.88), kind=kOutput, calls=%fused_computation.109 | convolution fusion | flops 67108864 | bytes 9961472 | tf_op jit(solution)/shard_map/pgs,psd->pgd/dot_general | solution.py:52
  199.8 4.7 %fusion.45 = f32[256,8,128]{2,1,0:T(8,128)S(1)} fusion(bf16[256,8,128]{2,1,0:T(8,128)(2,1)S(1)} %copy.101, bf16[256,128,128]{2,1,0:T(8,128)(2,1)} %reshape.271), kind=kOutput, calls=%fused_computation.110 | convolution fusion | flops 67108864 | bytes 9961472 | tf_op jit(solution)/shard_map/pgs,psd->pgd/dot_general | solution.py:52
  205.5 2.0 collective-permute-start.2
  207.5 1.6 collective-permute-done.3
  209.2 5.3 %fusion.25 = f32[4,8192]{1,0:T(4,128)} fusion(bf16[512,8192]{1,0:T(8,128)(2,1)} %param.23, f32[4,4,128]{2,0,1:T(4,128)S(1)} %collective-permute-done.2, f32[4,8,128]{2,0,1:T(4,128)S(1)} %fusion.3, s32[]{:T(128)S(6)} %select_n.152, f32[4,4]{0,1:T(4,128)S(1)} %copy.104), kind=kOutput, calls=%fused_computation.60 | convolution fusion | flops 33560576 | bytes 8538116 | tf_op jit(solution)/shard_map/dot_general | solution.py:179
  215.3 86.1 %all-reduce.4.cloned.1.call-done = f32[4,8192]{1,0:T(4,128)} async-done(((f32[4,8192]{1,0:T(4,128)}), f32[4,8192]{1,0:T(4,128)}) %all-reduce.4.cloned.1.call-update) | async-done | bytes 131088 | tf_op jit(solution)/shard_map/psum | solution.py:182
  301.4 1.1 multiply_reduce_fusion
  (93 shorter events, 12.4 us)
Async XLA Ops:
  6.5 63.2 %copy-start = (bf16[4,8,2,128]{3,2,1,0:T(2,128)(2,1)S(1)}, bf16[4,8,2,128]{3,2,1,0:T(2,128)(2,1)}, u32[]{:S(2)}) copy-start(bf16[4,8,2,128]{3,2,1,0:T(2,128)(2,1)} %param.22) | copy-start | bytes 49156
  47.7 11.8 %copy-start.5 = (bf16[4,512]{1,0:T(4,128)(2,1)S(1)}, bf16[4,512]{1,0:T(4,128)(2,1)}, u32[]{:S(2)}) copy-start(bf16[4,512]{1,0:T(4,128)(2,1)} %param.21) | copy-start | bytes 12292
  47.7 13.0 %copy-start.7 = (s32[1,4]{1,0:T(1,128)S(1)}, s32[1,4]{1,0:T(1,128)}, u32[]{:S(2)}) copy-start(s32[1,4]{1,0:T(1,128)} %param.19) | copy-start | bytes 52
  47.7 13.4 %copy-start.4 = (s32[768]{0:T(1024)S(1)}, s32[768]{0:T(1024)}, u32[]{:S(2)}) copy-start(s32[768]{0:T(1024)} %param.16) | copy-start | bytes 9220
  47.7 13.7 %copy-start.6 = (s32[1,256]{1,0:T(1,128)S(1)}, s32[1,256]{1,0:T(1,128)}, u32[]{:S(2)}) copy-start(s32[1,256]{1,0:T(1,128)} %param.18) | copy-start | bytes 3076
  47.7 15.1 %copy-start.2 = (s32[1,256]{1,0:T(1,128)S(1)}, s32[1,256]{1,0:T(1,128)}, u32[]{:S(2)}) copy-start(s32[1,256]{1,0:T(1,128)} %param.17) | copy-start | bytes 3076
  47.7 20.8 %copy-start.8 = (s32[4]{0:T(128)S(1)}, s32[4]{0:T(128)}, u32[]{:S(2)}) copy-start(s32[4]{0:T(128)} %param.20) | copy-start | bytes 52
  47.7 115.6 %all-to-all-start = ((bf16[128,2,16384]{2,1,0:T(2,128)(2,1)}), bf16[128,2,16384]{2,1,0:T(2,128)(2,1)}, u32[]{:S(2)}, u32[]{:S(2)}) async-start(bf16[128,2,16384]{2,1,0:T(2,128)(2,1)} %copy.95), calls=%async_computation | async-start | bytes 16777216 | tf_op jit(solution)/shard_map/all_to_all | solution.py:98
  59.4 241.9 %all-reduce.4.cloned.1.call-start = ((), (), s32[]{:S(2)}) async-start(), calls=%async_computation.1 | async-start | bytes 262144 | tf_op jit(solution)/shard_map/psum | solution.py:182
  59.5 95.4 %collective-permute-start = (bf16[4,512]{1,0:T(4,128)(2,1)S(1)}, bf16[4,512]{1,0:T(4,128)(2,1)S(1)}, u32[]{:S(2)}, u32[]{:S(2)}) collective-permute-start(bf16[4,512]{1,0:T(4,128)(2,1)S(1)} %copy-done.5), channel_id=1, source_target_pairs={{0,1},{1,0},{2,3},{3,2},{4,5},{5,4},{6,7},{7,6},{8,9},{9,8},{10,11... | collective-permute-start | bytes 12296 | tf_op jit(solution)/shard_map/ppermute | solution.py:19
  187.6 3.9 %collective-permute-start.1 = (f32[4,8]{1,0:T(4,128)S(1)}, f32[4,8]{1,0:T(4,128)S(1)}, u32[]{:S(2)}, u32[]{:S(2)}) collective-permute-start(f32[4,8]{1,0:T(4,128)S(1)} %maximum_maximum_fusion), channel_id=1, source_target_pairs={{0,1},{1,0},{2,3},{3,2},{4,5},{5,4},{6,7},{7,6},{8,9},{9,8},{10,11... | collective-permute-start | bytes 392 | tf_op jit(solution)/shard_map/ppermute | solution.py:19
  199.8 103.3 %copy-start.1 = (bf16[4,8,2,128]{3,2,1,0:T(2,128)(2,1)S(1)}, bf16[4,8,2,128]{3,2,1,0:T(2,128)(2,1)}, u32[]{:S(2)}) copy-start(bf16[4,8,2,128]{3,2,1,0:T(2,128)(2,1)} %param.22) | copy-start | bytes 49156
  204.5 96.9 %copy-start.3 = (bf16[4,8192]{1,0:T(4,128)(2,1)S(1)}, bf16[4,8192]{1,0:T(4,128)(2,1)}, u32[]{:S(2)}) copy-start(bf16[4,8192]{1,0:T(4,128)(2,1)} %param.24) | copy-start | bytes 196612
  205.4 3.6 %collective-permute-start.3 = (f32[4,4]{1,0:T(4,128)S(1)}, f32[4,4]{1,0:T(4,128)S(1)}, u32[]{:S(2)}, u32[]{:S(2)}) collective-permute-start(f32[4,4]{1,0:T(4,128)S(1)} %constant_dynamic-slice_fusion), channel_id=1, source_target_pairs={{0,1},{1,0},{2,3},{3,2},{4,5},{5,4},{6,7},{7,6},{8,9},{9,8},{10,11... | collective-permute-start | bytes 200 | tf_op jit(solution)/shard_map/ppermute | solution.py:19
  205.5 3.7 %collective-permute-start.2 = (f32[4,4,128]{2,0,1:T(4,128)S(1)}, f32[4,4,128]{2,0,1:T(4,128)S(1)}, u32[]{:S(2)}, u32[]{:S(2)}) collective-permute-start(f32[4,4,128]{2,0,1:T(4,128)S(1)} %constant_dynamic-slice_fusion.1), channel_id=1, source_target_pairs={{0,1},{1,0},{2,3},{3,2},{4,5},{5,4},{6,7},{7,6},{8,9},{9,8},{10,11... | collective-permute-start | bytes 24584 | tf_op jit(solution)/shard_map/ppermute | solution.py:19
Sparse Core Ops, SparseCore 0:
  214.6 86.6 all-reduce.3
where the time goes:
time: 311 us; the launch traced here: 310 us
  waiting for transfers between devices  176 us (57%)
  local copies, waits for them, and re-layouts  61.3 us (20%)
  matrix products  37.4 us (12%)
  starting transfers between devices  15.2 us (5%)
  between operations  13.9 us (4%)
  other arithmetic  5.89 us (2%)
    ppermute x4, waiting for transfers between devices, partner(): return lax.ppermute(block, axis, route)  90.2 us
    psum x1, waiting for transfers between devices, local(): projected = lax.psum(partial_sum, 'tensor')  86.1 us
    reshape x1, local copies, waits for them, and re-layouts, local(): sectioning = sectioning.reshape(dp_count * tp_count, CAPACITY, piece_size)  16.3 us
    reshape x1, local copies, waits for them, and re-layouts, local(): arrival_blocks = received.reshape(-1, 2 * half_tokens, head_dim)  14.5 us
    dot_general x2, matrix products, block_scores(): jnp.einsum('pgd,psd->pgs', slot_query, blocks, preferred_element_type=jnp...  13.5 us
    all_to_all x1, starting transfers between devices, local(): lax.all_to_all(sectioning, ('dp', 'tensor'), split_axis=0, concat_axis=0,...  11.7 us
    convert_element_type x1, local copies, waits for them, and re-layouts, local(): sectioning = jnp.einsum('dcf,ftr->dtcr', picker, flat_blocks, preferred_e...  11.2 us
    dot_general x2, matrix products, block_sums(): jnp.einsum('pgs,psd->pgd', spaced, blocks, preferred_element_type=jnp.flo...  9.33 us
  transfers between devices with their start and end apart: 6, of which 4 were waited for; matrix products, arithmetic and copies ran while one was open for 6% of the time, Pallas kernels for 0%

commit v1 on v0

v1 whole, which is shorter than its diff:
```python
import functools
import math

import jax
import jax.numpy as jnp
from jax import lax
from jax.experimental import pallas as pl
from jax.experimental.pallas import tpu as pltpu
from jax.sharding import PartitionSpec as P

MESH = pl.DeviceIdType.MESH
ROWS = 4
OWN = 4
OCTET = 8
HD = 128
BLOCK_TOKENS = 128
HALF = BLOCK_TOKENS // 2
CAPACITY = 2
NEG = -1e30
FACTOR = math.log2(math.e) / math.sqrt(HD)
POOL_CHUNK = 16


def dot_nt(a, b):
    return lax.dot_general(a, b, (((1,), (1,)), ((), ())), preferred_element_type=jnp.float32)


def dot_nn(a, b):
    return jnp.dot(a, b, preferred_element_type=jnp.float32)


def kernel(
    dp_n, tp_n, fresh_n, block_n,
    pool_hbm, fresh_hbm, w_hbm,
    routes_s, counts_s, tail_s, routes_v, landing_v, order_v, queries_v, new_kv_v, residual_v,
    out_ref,
    pool_v, fresh_v, w_v, scores, lim, qf, q_all, q_mate, meta, facc, stat, stat_t,
    tx1, tx1s, rx1, rx1s, tx2, rx2, att, tx3, rx3, tx4, rx4,
    pool_sem, fresh_sem, w_sem,
    mate_send, mate_recv, a1_send, a1_recv, am_send, am_recv, a2_send, a2_recv,
    c1_send, c1_recv, c1s_send, c1s_recv, c2_send, c2_recv, d_send, d_recv, e_send, e_recv,
):
    d = lax.axis_index("dp")
    t = lax.axis_index("tensor")
    source = d * tp_n + t
    head_n = OWN * tp_n
    kv_n = tp_n // 2
    kv = t // 2
    half = t % 2
    mate = t + 1 - 2 * half
    rows_of_chunk = POOL_CHUNK * BLOCK_TOKENS
    chunk_n = block_n // POOL_CHUNK

    def pool_copy(c):
        at = pl.ds(pl.multiple_of(c * rows_of_chunk, rows_of_chunk), rows_of_chunk)
        return pltpu.make_async_copy(pool_hbm.at[at], pool_v.at[at], pool_sem.at[c])

    def fresh_copy(i):
        size = 2 * kv_n * BLOCK_TOKENS
        at = pl.ds(pl.multiple_of(i * size, size), size)
        return pltpu.make_async_copy(fresh_hbm.at[at], fresh_v.at[at], fresh_sem.at[i])

    def w_copy(i):
        size = OWN * HD // 4
        at = pl.ds(pl.multiple_of(i * size, size), size)
        return pltpu.make_async_copy(w_hbm.at[at], w_v.at[at], w_sem.at[i])

    def start_all(n, copy):
        def body(i, carry):
            copy(i).start()
            return carry

        lax.fori_loop(0, n, body, 0)

    start_all(chunk_n, pool_copy)
    start_all(fresh_n, fresh_copy)
    start_all(4, w_copy)

    barrier = pltpu.get_barrier_semaphore()

    def greet_dp(j, carry):
        pl.semaphore_signal(barrier, 1, device_id=(lax.rem(d + j, dp_n), t), device_id_type=MESH)
        return carry

    def greet_tp(j, carry):
        pl.semaphore_signal(barrier, 1, device_id=(d, lax.rem(t + j, tp_n)), device_id_type=MESH)
        return carry

    lax.fori_loop(1, dp_n, greet_dp, 0)
    lax.fori_loop(1, tp_n, greet_tp, 0)

    for h in range(OWN):
        qf[pl.ds(h, ROWS, stride=OWN), :] = queries_v[:, h * HD : (h + 1) * HD].astype(jnp.float32)
    q_own = qf[...]
    q_all[t, d] = q_own.astype(jnp.bfloat16)

    place = lax.broadcasted_iota(jnp.int32, (1, block_n), 1)
    row_of = jnp.zeros((1, block_n), jnp.int32)
    reach = jnp.zeros((1, block_n), jnp.int32)
    start = jnp.int32(0)
    for r in range(ROWS):
        count = counts_s[r]
        end = start + count
        inside = (place >= start) & (place < end)
        row_of = jnp.where(inside, r, row_of)
        reach = jnp.where(inside, (end - 1) * BLOCK_TOKENS + tail_s[r], reach)
        start = end
    limit = jnp.clip(reach - place * BLOCK_TOKENS, 0, BLOCK_TOKENS)
    code = (row_of * 256 + limit).astype(jnp.float32)
    block_id = lax.broadcasted_iota(jnp.int32, (block_n, block_n), 0)
    code_b = jnp.sum(jnp.where(order_v[...] == block_id, code, 0.0), axis=1, keepdims=True)
    route_n = routes_v.shape[1]
    mine = jnp.where(routes_v[...] == d, 1.0, 0.0)
    mine = jnp.broadcast_to(mine, (8, route_n)).astype(jnp.bfloat16)
    first = lax.broadcasted_iota(jnp.int32, (route_n, block_n), 1) // CAPACITY * fresh_n
    entry = lax.broadcasted_iota(jnp.int32, (route_n, block_n), 0)
    spread = jnp.where((entry >= first) & (entry < first + fresh_n), 1.0, 0.0).astype(jnp.bfloat16)
    sent = dot_nn(mine, spread)[0:1]
    arrived = jnp.where((place % CAPACITY).astype(jnp.float32) < sent, 1.0, 0.0)
    lands = landing_v[...] == block_id
    replaced = jnp.sum(jnp.where(lands, arrived, 0.0), axis=1, keepdims=True)
    table = jnp.sum(jnp.where(lands, code_b, 0.0), axis=0, keepdims=True)
    meta[d] = jnp.broadcast_to(table, (8, block_n))

    pl.semaphore_wait(barrier, dp_n + tp_n - 2)

    def a1(j):
        to = lax.rem(d + j, dp_n)
        return pltpu.make_async_remote_copy(
            q_all.at[t, d], q_all.at[t, d], a1_send.at[j], a1_recv.at[j],
            device_id=(to, t), device_id_type=MESH,
        )

    def am(j):
        to = lax.rem(d + j, dp_n)
        return pltpu.make_async_remote_copy(
            meta.at[d], meta.at[d], am_send.at[j], am_recv.at[j],
            device_id=(to, t), device_id_type=MESH,
        )

    def a1_from(j):
        come = lax.rem(d + dp_n - j, dp_n)
        return pltpu.make_async_remote_copy(
            q_all.at[t, come], q_all.at[t, come], a1_send.at[j], a1_recv.at[j],
            device_id=(come, t), device_id_type=MESH,
        )

    def am_from(j):
        come = lax.rem(d + dp_n - j, dp_n)
        return pltpu.make_async_remote_copy(
            meta.at[come], meta.at[come], am_send.at[j], am_recv.at[j],
            device_id=(come, t), device_id_type=MESH,
        )

    def a2(j):
        to = lax.rem(t + j, tp_n)
        return pltpu.make_async_remote_copy(
            q_all.at[t], q_all.at[t], a2_send.at[j], a2_recv.at[j],
            device_id=(d, to), device_id_type=MESH,
        )

    def a2_from(j):
        come = lax.rem(t + tp_n - j, tp_n)
        return pltpu.make_async_remote_copy(
            q_all.at[come], q_all.at[come], a2_send.at[j], a2_recv.at[j],
            device_id=(d, come), device_id_type=MESH,
        )

    def loop(first_j, end_j, act):
        def body(j, carry):
            act(j)
            return carry

        lax.fori_loop(first_j, end_j, body, 0)

    to_mate = pltpu.make_async_remote_copy(
        q_all.at[t, d], q_mate, mate_send, mate_recv, device_id=(d, mate), device_id_type=MESH
    )
    to_mate.start()
    loop(1, dp_n, lambda j: a1(j).start())
    loop(1, dp_n, lambda j: am(j).start())

    code_live = jnp.where(replaced > 0.0, 0.0, code_b)
    for r in range(ROWS):
        tokens = code_live - 256.0 * r
        tokens = jnp.where((tokens > 0.0) & (tokens <= float(BLOCK_TOKENS)), tokens, 0.0)
        tokens = jnp.clip(tokens - (half * HALF).astype(jnp.float32), 0.0, float(HALF))
        lim[r] = jnp.broadcast_to(2.0 * tokens, (block_n, HD))

    to_mate.wait_recv()
    q_other = q_mate[...].astype(jnp.float32)
    low = jnp.where(half == 0, q_own, q_other)
    high = jnp.where(half == 0, q_other, q_own)
    sub = lax.broadcasted_iota(jnp.int32, (8, HD), 0)
    lane = lax.broadcasted_iota(jnp.int32, (8, HD), 1)
    parts = []
    for r in range(ROWS):
        a = low[8 * (r // 2) : 8 * (r // 2) + 8]
        b = high[8 * (r // 2) : 8 * (r // 2) + 8]
        if r % 2 == 0:
            b = pltpu.roll(b, 4, 0)
        else:
            a = pltpu.roll(a, 4, 0)
        parts.append(jnp.where(sub < 4, a, b))
    q_pool = jnp.concatenate(parts, axis=0).astype(jnp.bfloat16)

    loop(1, dp_n, lambda j: a1_from(j).wait_recv())
    loop(1, tp_n, lambda j: a2(j).start())
    loop(1, dp_n, lambda j: am_from(j).wait_recv())

    even_lane = jnp.where(lane % 2 == 0, lane, 1 << 20).astype(jnp.float32)

    def pool_scores(c, tops):
        pool_copy(c).wait()
        base = pl.multiple_of(c * rows_of_chunk, rows_of_chunk)
        s = dot_nt(q_pool, pool_v[pl.ds(base, rows_of_chunk), :])
        tops = list(tops)
        for j in range(POOL_CHUNK):
            for r in range(ROWS):
                bound = jnp.broadcast_to(lim[r, pl.ds(c * POOL_CHUNK + j, 1), :], (8, HD))
                piece = s[8 * r : 8 * r + 8, j * HD : (j + 1) * HD]
                piece = jnp.where(even_lane < bound, piece, NEG)
                tops[r] = jnp.maximum(tops[r], piece)
                scores[8 * r : 8 * r + 8, pl.ds(base + j * HD, HD)] = piece
        return tuple(tops)

    tops = lax.fori_loop(0, chunk_n, pool_scores, (jnp.full((8, HD), NEG, jnp.float32),) * ROWS)
    pool_top = [jnp.maximum(jnp.max(x, axis=1, keepdims=True), 0.1 * NEG) for x in tops]

    loop(1, tp_n, lambda j: a2_from(j).wait_recv())
    wide = lax.broadcasted_iota(jnp.int32, (8, 2 * HD), 1)
    token = jnp.where(wide % 2 == 0, wide // 2, 1 << 20).astype(jnp.float32)
    wide_place = lax.broadcasted_iota(jnp.int32, (8, block_n), 1)
    stat[...] = jnp.zeros_like(stat)
    first_own = source * fresh_n

    def rank_of(i):
        rank = jnp.int32(0)
        for j in range(fresh_n):
            same = (routes_s[first_own + j] == routes_s[first_own + i]) & (j < i)
            rank = rank + same.astype(jnp.int32)
        return rank

    def fresh_block(i, carry):
        fresh_copy(i).wait()
        group = routes_s[first_own + i]
        arrival = source * CAPACITY + rank_of(i)
        found = jnp.sum(
            jnp.where(wide_place == arrival, meta[group], 0.0), axis=1, keepdims=True
        )
        row = jnp.where(found >= 256.0, 1.0, 0.0) + jnp.where(found >= 512.0, 1.0, 0.0)
        row = row + jnp.where(found >= 768.0, 1.0, 0.0)
        live = found - 256.0 * row
        upper = jnp.broadcast_to(row >= 2.0, (8, HD))
        odd = jnp.broadcast_to((row == 1.0) | (row == 3.0), (8, HD))
        seen = token < live
        for k in range(kv_n):
            picks = []
            for side in range(2):
                tile = q_all[2 * k + side, group].astype(jnp.float32)
                v = jnp.where(upper, tile[8:16], tile[0:8])
                u = pltpu.roll(v, 4, 0)
                picks.append(jnp.where(odd, u, v) if side == 0 else jnp.where(odd, v, u))
            q_k = jnp.where(sub < 4, picks[0], picks[1]).astype(jnp.bfloat16)
            base = pl.multiple_of((i * kv_n + k) * 2 * BLOCK_TOKENS, 2 * BLOCK_TOKENS)
            x = fresh_v[pl.ds(base, 2 * BLOCK_TOKENS), :]
            s = jnp.where(seen, dot_nt(q_k, x), NEG)
            top = jnp.max(s, axis=1, keepdims=True)
            p = jnp.exp2((s - top) * FACTOR)
            total = jnp.sum(p, axis=1, keepdims=True)
            p = jnp.concatenate([pltpu.roll(p[:, :HD], 1, 1), pltpu.roll(p[:, HD:], 1, 1)], axis=1)
            facc[i, 8 * k : 8 * k + 8, :] = dot_nn(p.astype(jnp.bfloat16), x)
            kept = stat[8 * k : 8 * k + 8, :]
            kept = jnp.where(lane == i, top, kept)
            kept = jnp.where(lane == 8 + i, total, kept)
            stat[8 * k : 8 * k + 8, :] = jnp.where(lane == 16 + i, row, kept)
        return carry

    lax.fori_loop(0, fresh_n, fresh_block, 0)
    stat_t[...] = jnp.transpose(stat[...])

    def pack(g, carry):
        for slot in range(CAPACITY):
            chosen = jnp.int32(0)
            hit = jnp.int32(0)
            for i in range(fresh_n):
                ok = ((routes_s[first_own + i] == g) & (rank_of(i) == slot)).astype(jnp.int32)
                chosen = chosen + ok * i
                hit = hit + ok
            there = hit > 0
            acc = facc[chosen]
            tx1[g, slot * head_n : (slot + 1) * head_n, :] = jnp.where(there, acc, 0.0).astype(
                jnp.bfloat16
            )
            tx1s[g, slot : slot + 1, :] = jnp.where(there, stat_t[pl.ds(chosen, 1), :], NEG)
            tx1s[g, 2 + slot : 3 + slot, :] = jnp.where(there, stat_t[pl.ds(8 + chosen, 1), :], 0.0)
            tx1s[g, 4 + slot : 5 + slot, :] = jnp.where(there, stat_t[pl.ds(16 + chosen, 1), :], 0.0)
        tx1s[g, 6:8, :] = jnp.zeros((2, HD), jnp.float32)
        return carry

    lax.fori_loop(0, dp_n, pack, 0)

    def c1(j):
        to = lax.rem(d + j, dp_n)
        return pltpu.make_async_remote_copy(
            tx1.at[to], rx1.at[d], c1_send.at[j], c1_recv.at[j],
            device_id=(to, t), device_id_type=MESH,
        )

    def c1s(j):
        to = lax.rem(d + j, dp_n)
        return pltpu.make_async_remote_copy(
            tx1s.at[to], rx1s.at[d], c1s_send.at[j], c1s_recv.at[j],
            device_id=(to, t), device_id_type=MESH,
        )

    def c1_from(j):
        come = lax.rem(d + dp_n - j, dp_n)
        return pltpu.make_async_remote_copy(
            tx1.at[come], rx1.at[come], c1_send.at[j], c1_recv.at[j],
            device_id=(come, t), device_id_type=MESH,
        )

    def c1s_from(j):
        come = lax.rem(d + dp_n - j, dp_n)
        return pltpu.make_async_remote_copy(
            tx1s.at[come], rx1s.at[come], c1s_send.at[j], c1s_recv.at[j],
            device_id=(come, t), device_id_type=MESH,
        )

    loop(1, dp_n, lambda j: c1s(j).start())
    loop(1, dp_n, lambda j: c1(j).start())
    rx1[d] = tx1[d]
    rx1s[d] = tx1s[d]

    def pool_values(c, carry):
        acc, sums = carry
        base = pl.multiple_of(c * rows_of_chunk, rows_of_chunk)
        sums = list(sums)
        columns = []
        for j in range(POOL_CHUNK):
            pieces = []
            for r in range(ROWS):
                piece = scores[8 * r : 8 * r + 8, pl.ds(base + j * HD, HD)]
                p = jnp.exp2((piece - pool_top[r]) * FACTOR)
                sums[r] = sums[r] + p
                pieces.append(pltpu.roll(p, 1, 1))
            columns.append(jnp.concatenate(pieces, axis=0).astype(jnp.bfloat16))
        p_all = jnp.concatenate(columns, axis=1)
        acc = acc + dot_nn(p_all, pool_v[pl.ds(base, rows_of_chunk), :])
        return acc, tuple(sums)

    pool_acc, sums = lax.fori_loop(
        0,
        chunk_n,
        pool_values,
        (jnp.zeros((8 * ROWS, HD), jnp.float32), (jnp.zeros((8, HD), jnp.float32),) * ROWS),
    )
    pool_sum = [jnp.sum(x, axis=1, keepdims=True) for x in sums]

    loop(1, dp_n, lambda j: c1s_from(j).wait_recv())
    loop(1, dp_n, lambda j: c1_from(j).wait_recv())
    stat[0 : 8 * dp_n, :] = rx1s[...].reshape(8 * dp_n, HD)
    stat_t[...] = jnp.transpose(stat[...])
    valid = (lane % 8 < CAPACITY) & (lane < 8 * dp_n)

    def c2(to):
        return pltpu.make_async_remote_copy(
            tx2.at[to], rx2.at[t], c2_send.at[to], c2_recv.at[t],
            device_id=(d, to), device_id_type=MESH,
        )

    def c2_from(come):
        return pltpu.make_async_remote_copy(
            tx2.at[come], rx2.at[come], c2_send.at[come], c2_recv.at[come],
            device_id=(d, come), device_id_type=MESH,
        )

    for m in range(kv_n):
        tops_in = stat_t[8 * m : 8 * m + 8, :]
        rows_in = pltpu.roll(tops_in, HD - 4, 1)
        sums_in = pltpu.roll(tops_in, HD - 2, 1)
        here = kv == m
        best = []
        top_of = jnp.zeros((8, HD), jnp.float32)
        for r in range(ROWS):
            of_row = valid & (rows_in == float(r))
            top = jnp.max(jnp.where(of_row, tops_in, NEG), axis=1, keepdims=True)
            top = jnp.maximum(top, jnp.where(here, pool_top[r], NEG))
            best.append(top)
            top_of = jnp.where(of_row, top, top_of)
        weight = jnp.where(valid, jnp.exp2((tops_in - top_of) * FACTOR), 0.0)
        mass = weight * sums_in
        accs = []
        masses = []
        for r in range(ROWS):
            w_pool = jnp.where(here, jnp.exp2((pool_top[r] - best[r]) * FACTOR), 0.0)
            accs.append(w_pool * pool_acc[8 * r : 8 * r + 8])
            share = jnp.sum(jnp.where(rows_in == float(r), mass, 0.0), axis=1, keepdims=True)
            masses.append(share + w_pool * pool_sum[r])
        for g in range(dp_n):
            for slot in range(CAPACITY):
                at = 8 * g + slot
                w = jnp.broadcast_to(weight[:, at : at + 1], (8, HD))
                row = jnp.broadcast_to(rows_in[:, at : at + 1], (8, HD))
                low_at = slot * head_n + 8 * m
                term = w * rx1[g, low_at : low_at + 8, :].astype(jnp.float32)
                for r in range(ROWS):
                    accs[r] = accs[r] + jnp.where(row == float(r), term, 0.0)
        stats = [jnp.where(lane < 64, best[r], masses[r]) for r in range(ROWS)]
        for group, at in ((accs, 0), (stats, 16)):
            for pair in range(2):
                a, b = group[2 * pair], group[2 * pair + 1]
                rows = slice(at + 8 * pair, at + 8 * pair + 8)
                tx2[2 * m, rows, :] = jnp.where(sub < 4, a, pltpu.roll(b, 4, 0))
                tx2[2 * m + 1, rows, :] = jnp.where(sub < 4, pltpu.roll(a, 4, 0), b)
        for to in (2 * m, 2 * m + 1):

            @pl.when(t != to)
            def _():
                c2(to).start()

    rx2[t] = tx2[t]

    new_rows = new_kv_v[...].astype(jnp.float32)
    att[...] = new_rows
    keys = []
    values = []
    for r in range(ROWS):
        at = (r * kv_n + kv) * 2
        keys.append(jnp.broadcast_to(att[pl.ds(at, 1), :], (OWN, HD)))
        values.append(jnp.broadcast_to(att[pl.ds(at + 1, 1), :], (OWN, HD)))
    key_new = jnp.concatenate(keys, axis=0)
    value_new = jnp.concatenate(values, axis=0)
    score_new = jnp.sum(q_own * key_new, axis=1, keepdims=True)

    def c2_wait(j, carry):
        c2_from(lax.rem(t + j, tp_n)).wait_recv()
        return carry

    lax.fori_loop(1, tp_n, c2_wait, 0)
    lane16 = lax.broadcasted_iota(jnp.int32, (16, HD), 1)
    top = jnp.broadcast_to(score_new, (16, HD))
    for j in range(tp_n):
        top = jnp.maximum(top, rx2[j, 16:32, :])
    top = jnp.where(lane16 < 64, top, pltpu.roll(top, 64, 1))
    weight = jnp.exp2((score_new - top) * FACTOR)
    acc = weight * value_new
    mass = weight
    for j in range(tp_n):
        their = rx2[j, 16:32, :]
        w = jnp.exp2((jnp.where(lane16 < 64, their, pltpu.roll(their, 64, 1)) - top) * FACTOR)
        acc = acc + w * rx2[j, 0:16, :]
        mass = mass + w * their
    mass = jnp.where(lane16 < 64, pltpu.roll(mass, 64, 1), mass)
    attended = acc / mass

    qf[...] = attended
    zeros = jnp.zeros((ROWS, OWN * HD), jnp.float32)
    flat = jnp.concatenate([qf[pl.ds(h, ROWS, stride=OWN), :] for h in range(OWN)], axis=1)
    first_rows = jnp.concatenate([flat, zeros], axis=0).astype(jnp.bfloat16)
    last_rows = jnp.concatenate([zeros, flat], axis=0).astype(jnp.bfloat16)
    loop(0, 4, lambda i: w_copy(i).wait())
    share = w_v.shape[1] // tp_n
    side = share // 2

    def d_send_copy(to):
        return pltpu.make_async_remote_copy(
            tx3.at[to], rx3.at[t], d_send.at[to], d_recv.at[t],
            device_id=(d, to), device_id_type=MESH,
        )

    def d_from(come):
        return pltpu.make_async_remote_copy(
            tx3.at[come], rx3.at[come], d_send.at[come], d_recv.at[come],
            device_id=(d, come), device_id_type=MESH,
        )

    def project(to):
        base = pl.multiple_of(to * share, share)
        return dot_nn(first_rows, w_v[:, pl.ds(base, side)]) + dot_nn(
            last_rows, w_v[:, pl.ds(base + side, side)]
        )

    def project_step(j, carry):
        to = lax.rem(t + j, tp_n)
        tx3[to] = project(to)
        d_send_copy(to).start()
        return carry

    lax.fori_loop(1, tp_n, project_step, 0)
    base = pl.multiple_of(t * share, share)
    res = jnp.concatenate(
        [residual_v[:, pl.ds(base, side)], residual_v[:, pl.ds(base + side, side)]], axis=0
    ).astype(jnp.float32)
    hidden = res + project(t)

    def d_wait(j, carry):
        d_from(lax.rem(t + j, tp_n)).wait_recv()
        return carry

    lax.fori_loop(1, tp_n, d_wait, 0)
    rx3[t] = hidden
    hidden = rx3[0]
    for j in range(1, tp_n):
        hidden = hidden + rx3[j]

    square = jnp.sum(hidden * hidden, axis=1, keepdims=True)
    square = jnp.broadcast_to(square, (8, HD))
    tx4[...] = square + pltpu.roll(square, 4, 0)

    def e_copy(to):
        return pltpu.make_async_remote_copy(
            tx4, rx4.at[t], e_send.at[to], e_recv.at[t],
            device_id=(d, to), device_id_type=MESH,
        )

    def e_from(come):
        return pltpu.make_async_remote_copy(
            tx4, rx4.at[come], e_send.at[come], e_recv.at[come],
            device_id=(d, come), device_id_type=MESH,
        )

    loop(1, tp_n, lambda j: e_copy(lax.rem(t + j, tp_n)).start())
    rx4[t] = tx4[...]
    loop(1, tp_n, lambda j: e_from(lax.rem(t + j, tp_n)).wait_recv())
    square = rx4[0]
    for j in range(1, tp_n):
        square = square + rx4[j]
    scale = lax.rsqrt(square / float(w_v.shape[1]) + 1e-5)
    out_ref[...] = hidden * jnp.concatenate([scale] * (side // HD), axis=1)

    to_mate.wait_send()
    loop(1, dp_n, lambda j: a1(j).wait_send())
    loop(1, dp_n, lambda j: am(j).wait_send())
    loop(1, tp_n, lambda j: a2(j).wait_send())
    loop(1, dp_n, lambda j: c1s(j).wait_send())
    loop(1, dp_n, lambda j: c1(j).wait_send())
    loop(1, tp_n, lambda j: c2(lax.rem(t + j, tp_n)).wait_send())
    loop(1, tp_n, lambda j: d_send_copy(lax.rem(t + j, tp_n)).wait_send())
    loop(1, tp_n, lambda j: e_copy(lax.rem(t + j, tp_n)).wait_send())


def local(
    dp_n, tp_n,
    pool, fresh_kv, routes, landing_order, pool_order, block_counts, tail_fill,
    queries, new_kv, w_out, residual, gain,
):
    block_n = pool.shape[0]
    fresh_n = fresh_kv.shape[0]
    kv_n = new_kv.shape[1]
    head_n = OWN * tp_n
    width = w_out.shape[1]
    share = width // tp_n
    side = share // 2
    f32, bf16 = jnp.float32, jnp.bfloat16
    pool_rows = pool.reshape(block_n * BLOCK_TOKENS, HD)
    fresh_rows = fresh_kv.reshape(fresh_n * 2 * kv_n * BLOCK_TOKENS, HD)
    hbm = pl.BlockSpec(memory_space=pl.ANY)
    smem = pl.BlockSpec(memory_space=pltpu.SMEM)
    vmem = pl.BlockSpec(memory_space=pltpu.VMEM)
    dma = pltpu.SemaphoreType.DMA
    normed = pl.pallas_call(
        functools.partial(kernel, dp_n, tp_n, fresh_n, block_n),
        out_shape=jax.ShapeDtypeStruct((8, side), f32),
        in_specs=[hbm] * 3 + [smem] * 3 + [vmem] * 6,
        out_specs=vmem,
        scratch_shapes=[
            pltpu.VMEM(pool_rows.shape, bf16),
            pltpu.VMEM(fresh_rows.shape, bf16),
            pltpu.VMEM(w_out.shape, bf16),
            pltpu.VMEM((8 * ROWS, block_n * BLOCK_TOKENS), f32),
            pltpu.VMEM((ROWS, block_n, HD), f32),
            pltpu.VMEM((ROWS * OWN, HD), f32),
            pltpu.VMEM((tp_n, dp_n, ROWS * OWN, HD), bf16),
            pltpu.VMEM((ROWS * OWN, HD), bf16),
            pltpu.VMEM((dp_n, 8, block_n), f32),
            pltpu.VMEM((fresh_n, head_n, HD), f32),
            pltpu.VMEM((HD, HD), f32),
            pltpu.VMEM((HD, HD), f32),
            pltpu.VMEM((dp_n, CAPACITY * head_n, HD), bf16),
            pltpu.VMEM((dp_n, 8, HD), f32),
            pltpu.VMEM((dp_n, CAPACITY * head_n, HD), bf16),
            pltpu.VMEM((dp_n, 8, HD), f32),
            pltpu.VMEM((tp_n, 32, HD), f32),
            pltpu.VMEM((tp_n, 32, HD), f32),
            pltpu.VMEM((ROWS * kv_n * 2, HD), f32),
            pltpu.VMEM((tp_n, 8, side), f32),
            pltpu.VMEM((tp_n, 8, side), f32),
            pltpu.VMEM((8, HD), f32),
            pltpu.VMEM((tp_n, 8, HD), f32),
            dma((block_n // POOL_CHUNK,)),
            dma((fresh_n,)),
            dma((4,)),
            dma(()),
            dma(()),
            *[dma((dp_n,))] * 4,
            *[dma((tp_n,))] * 2,
            *[dma((dp_n,))] * 4,
            *[dma((tp_n,))] * 6,
        ],
        compiler_params=pltpu.CompilerParams(
            collective_id=0, has_side_effects=True, vmem_limit_bytes=48 << 20
        ),
    )(
        pool_rows,
        fresh_rows,
        w_out,
        routes,
        block_counts.reshape(-1),
        tail_fill,
        routes.reshape(1, -1),
        landing_order,
        pool_order,
        queries,
        new_kv.reshape(-1, HD),
        residual,
    )
    spot = lax.axis_index("tensor") * share
    gains = lax.dynamic_slice_in_dim(gain, spot, share, 0)
    flat = jnp.concatenate([normed[:ROWS], normed[ROWS:]], axis=1)
    return (flat * gains).astype(bf16)


def solution(mesh):
    return jax.shard_map(
        functools.partial(local, mesh.shape["dp"], mesh.shape["tensor"]),
        mesh=mesh,
        in_specs=(
            P("dp", "tensor", None, None, None),
            P(("dp", "tensor"), None, None, None, None),
            P(),
            P("dp", None),
            P("dp", None),
            P("dp", None),
            P("dp"),
            P("dp", "tensor"),
            P("dp", None, None, None),
            P("tensor", None),
            P("dp", None),
            P(),
        ),
        out_specs=P("dp", "tensor"),
        check_vma=False,
    )
```

time: 311 us -> 75.7 us (0.24)
  waiting for transfers between devices: 176 us -> 0 us
  Pallas kernels: 0 us -> 65.7 us
  local copies, waits for them, and re-layouts: 61.3 us -> 8.94 us
  matrix products: 37.4 us -> 0 us
  starting transfers between devices: 15.2 us -> 0 us
  between operations: 13.9 us -> 0.03 us
  other arithmetic: 5.89 us -> 0.6 us
    ppermute x4 -> x0, waiting for transfers between devices: 90.2 us -> none  [partner(): return lax.ppermute(block, axis, route)]
    psum x1 -> x0, waiting for transfers between devices: 86.1 us -> none  [local(): projected = lax.psum(partial_sum, 'tensor')]
    pallas_call x0 -> x1, Pallas kernels: none -> 65.7 us  [local(): pl.pallas_call(functools.partial(kernel, dp_n, tp_n, fresh_n, block_n), o...]
    dot_general x13 -> x0, matrix products: 37.4 us -> none  [the longest x2 13.5 us: block_scores(): jnp.einsum('pgd,psd->pgs', slot_query, blocks, preferred_element_type=jnp...]
    reshape x6 -> x1, local copies, waits for them, and re-layouts: 36.9 us -> 0.69 us  [local(): routes.reshape(1, -1)]
    all_to_all x1 -> x0, starting transfers between devices: 11.7 us -> none  [local(): lax.all_to_all(sectioning, ('dp', 'tensor'), split_axis=0, concat_axis=0,...]
    convert_element_type x2 -> x0, local copies, waits for them, and re-layouts: 11.4 us -> none  [the longest x1 11.2 us: local(): sectioning = jnp.einsum('dcf,ftr->dtcr', picker, flat_blocks, preferred_e...]
    unnamed x18, local copies, waits for them, and re-layouts: 0.05 us -> 7.48 us
  transfers between devices with their start and end apart: 6 -> 0, of which waited for: 4 -> 0; matrix products, arithmetic and copies ran while one was open for 6% -> 0% of each run, Pallas kernels for 0% -> 0%
where the time goes in v1:
time: 75.7 us; the launch traced here: 75.3 us
  Pallas kernels  65.7 us (87%)
  local copies, waits for them, and re-layouts  8.94 us (12%)
    pallas_call x1, Pallas kernels, local(): pl.pallas_call(functools.partial(kernel, dp_n, tp_n, fresh_n, block_n), o...  65.7 us
    unnamed x18, local copies, waits for them, and re-layouts  7.48 us

profile of v1, /device:TPU:0, one launch (start us, length us, event | category | flops | bytes accessed | tf_op | source)
XLA Modules:
  0.0 75.3 jit_solution(6426620585756613592)
XLA Ops:
  0.0 0.7 reshape.19.routes_v
  0.7 0.0 copy-start
  0.7 1.9 %copy-done = bf16[6,16,64,2,128]{4,3,2,1,0:T(2,128)(2,1)S(1)} copy-done((bf16[6,16,64,2,128]{4,3,2,1,0:T(2,128)(2,1)S(1)}, bf16[6,16,64,2,128]{4,3,2,1,0:T(2,128)(2,1)}, u32[]{:S(2)}) %copy-start) | copy-done | bytes 3145752
  2.6 0.0 copy-start.1
  2.6 0.8 %copy-done.1 = bf16[4,8192]{1,0:T(4,128)(2,1)S(1)} copy-done((bf16[4,8192]{1,0:T(4,128)(2,1)S(1)}, bf16[4,8192]{1,0:T(4,128)(2,1)}, u32[]{:S(2)}) %copy-start.1) | copy-done | bytes 65560
  3.4 0.0 copy-start.2
  3.4 0.7 copy-done.2
  4.1 0.0 copy-start.3
  4.1 0.7 copy-done.3
  4.8 0.0 copy-start.4
  4.8 0.7 copy-done.4
  5.5 0.0 copy-start.5
  5.5 0.7 copy-done.5
  6.2 0.0 copy-start.6
  6.2 0.7 copy-done.6
  6.9 0.0 copy-start.7
  6.9 0.7 copy-done.7
  7.5 0.0 copy-start.8
  7.5 0.7 copy-done.8
  8.2 65.7 %shard_map.118 = f32[8,256]{1,0:T(8,128)S(1)} custom-call(bf16[32768,128]{1,0:T(8,128)(2,1)} %bitcast.7, bf16[12288,128]{1,0:T(8,128)(2,1)S(1)} %bitcast.4, bf16[512,8192]{1,0:T(8,128)(2,1)} %w_hbm.1, s32[768]{0:T(1024)S(1)} %copy-done.3, s32[4]{0:T(128)S(1)} %bitcast.6, s32[4]{0:T(128)S(1)} %copy-done.8, s32[1,768]{1,0:T(1,128)S(1)} %reshape.19.routes_v, ...), custom_call_target="tpu_custom_call" | custom-call | tf_op jit(solution)/shard_map/pallas_call | solution.py:563
  74.0 0.8 %dynamic_slice.3 = f32[512]{0:T(512)S(1)} dynamic-slice(f32[8192]{0:T(1024)} %param.23, s32[]{:T(128)S(6)} %select_n.3), dynamic_slice_sizes={512} | dynamic-slice | bytes 4100 | tf_op jit(solution)/shard_map/dynamic_slice | solution.py:620
  74.7 0.6 fusion
  (1 shorter events, 0.0 us)
Async XLA Ops:
  0.7 1.9 %copy-start = (bf16[6,16,64,2,128]{4,3,2,1,0:T(2,128)(2,1)S(1)}, bf16[6,16,64,2,128]{4,3,2,1,0:T(2,128)(2,1)}, u32[]{:S(2)}) copy-start(bf16[6,16,64,2,128]{4,3,2,1,0:T(2,128)(2,1)} %param.13) | copy-start | bytes 9437188
  2.6 0.8 %copy-start.1 = (bf16[4,8192]{1,0:T(4,128)(2,1)S(1)}, bf16[4,8192]{1,0:T(4,128)(2,1)}, u32[]{:S(2)}) copy-start(bf16[4,8192]{1,0:T(4,128)(2,1)} %residual_v.1) | copy-start | bytes 196612
  3.4 0.7 copy-start.2
  4.1 0.7 copy-start.3
  4.8 0.7 copy-start.4
  5.5 0.7 copy-start.5
  6.2 0.7 copy-start.6
  6.9 0.7 copy-start.7
  7.5 0.7 copy-start.8

commit v2 on v1

v2 whole, which is shorter than its diff:
```python
import functools
import math

import jax
import jax.numpy as jnp
from jax import lax
from jax.experimental import pallas as pl
from jax.experimental.pallas import tpu as pltpu
from jax.sharding import PartitionSpec as P

MESH = pl.DeviceIdType.MESH
ROWS = 4
OWN = 4
HD = 128
BLOCK_TOKENS = 128
HALF = BLOCK_TOKENS // 2
CAPACITY = 2
NEG = -1e30
FACTOR = math.log2(math.e) / math.sqrt(HD)
POOL_CHUNK = 16
F32, BF16 = jnp.float32, jnp.bfloat16


def dot_nt(a, b):
    return lax.dot_general(a, b, (((1,), (1,)), ((), ())), preferred_element_type=F32)


def dot_nn(a, b):
    return jnp.dot(a, b, preferred_element_type=F32)


def iota(shape, axis):
    return lax.broadcasted_iota(jnp.int32, shape, axis)


def split(x):
    high = x.astype(BF16).astype(F32)
    return high, x - high


def kernel(
    dp_n, tp_n, fresh_n, block_n,
    pool_hbm, fresh_hbm, w_hbm, routes_hbm, counts_hbm, tail_hbm, landing_hbm, order_hbm,
    queries_hbm, new_kv_hbm, residual_hbm, gain_hbm,
    out_ref,
    routes_s, counts_s, tail_s, routes_v, landing_v, order_v, queries_v, new_kv_v, residual_v, gain_v,
    pool_v, fresh_v, w_v, scores, lim, qf, q_own_v, q_mate, new_kv_f,
    tx0, rx0, picks, rx1, fscore, facc, stat, stat_t, rows_top, rows_sum,
    txc, rxc, tx2, rx2, tx3, rx3, tx4, rx4,
    small_sem, pool_sem, fresh_sem, w_sem,
    mate_send, mate_recv, a1_send, a1_recv, a2_send, a2_recv,
    c1_send, c1_recv, c2_send, c2_recv, d_send, d_recv, e_send, e_recv,
):
    d = lax.axis_index("dp")
    t = lax.axis_index("tensor")
    source = d * tp_n + t
    kv_n = tp_n // 2
    kv = t // 2
    half = t % 2
    mate = t + 1 - 2 * half
    rows_of_chunk = POOL_CHUNK * BLOCK_TOKENS
    chunk_n = block_n // POOL_CHUNK
    route_n = routes_hbm.shape[0]
    plane_n = tp_n * fresh_n
    tp_side = math.isqrt(tp_n)
    width = w_v.shape[1]
    share = width // tp_n
    side = share // 2

    def dp_partner(dz, dc):
        return lax.rem(d // 2 + dz, dp_n // 2) * 2 + lax.rem(d + dc, 2)

    def tp_partner(dx, dy):
        return lax.rem(t // tp_side + dx, tp_side) * tp_side + lax.rem(t + dy, tp_side)

    def far(a, n):
        return min(a, n - a)

    dp_steps = [(dz, dc) for dz in range(dp_n // 2) for dc in range(2) if dz or dc]
    dp_steps.sort(key=lambda s: -far(s[0], dp_n // 2))
    tp_steps = [(dx, dy) for dx in range(tp_side) for dy in range(tp_side) if dx or dy]
    tp_steps.sort(key=lambda s: -far(s[0], tp_side) - far(s[1], tp_side))
    dp_partners = [dp_partner(*s) for s in dp_steps]
    tp_partners = [tp_partner(*s) for s in tp_steps]

    def loop(first_j, end_j, act):
        def body(j, carry):
            act(j)
            return carry

        lax.fori_loop(first_j, end_j, body, 0)

    def each_dp(act):
        loop(1, dp_n, lambda j: act(lax.rem(d + j, dp_n)))

    def each_tp(act):
        loop(1, tp_n, lambda j: act(lax.rem(t + j, tp_n)))

    at_share = pl.ds(pl.multiple_of(t * share, share), share)
    small = [
        (queries_hbm, queries_v),
        (routes_hbm, routes_v),
        (landing_hbm, landing_v),
        (order_hbm, order_v),
        (counts_hbm, counts_s),
        (tail_hbm, tail_s),
        (routes_hbm, routes_s),
        (new_kv_hbm, new_kv_v),
        (residual_hbm.at[:, at_share], residual_v),
        (gain_hbm, gain_v),
    ]
    small = [pltpu.make_async_copy(a, b, small_sem.at[i]) for i, (a, b) in enumerate(small)]
    for copy in small:
        copy.start()

    barrier = pltpu.get_barrier_semaphore()
    for to in tp_partners:
        pl.semaphore_signal(barrier, 1, device_id=(d, to), device_id_type=MESH)
    for to in dp_partners:
        pl.semaphore_signal(barrier, 1, device_id=(to, t), device_id_type=MESH)

    def pool_copy(c):
        at = pl.ds(pl.multiple_of(c * rows_of_chunk, rows_of_chunk), rows_of_chunk)
        return pltpu.make_async_copy(pool_hbm.at[at], pool_v.at[at], pool_sem.at[c])

    fresh_copy = pltpu.make_async_copy(fresh_hbm, fresh_v, fresh_sem)
    w_copy = pltpu.make_async_copy(w_hbm, w_v, w_sem)
    loop(0, chunk_n, lambda c: pool_copy(c).start())
    fresh_copy.start()
    w_copy.start()

    sub = iota((8, HD), 0)
    lane = iota((8, HD), 1)
    small[0].wait()
    for h in range(OWN):
        qf[pl.ds(h, ROWS, stride=OWN), :] = queries_v[:, h * HD : (h + 1) * HD].astype(F32)
    q_own = qf[...]
    q_own_v[...] = q_own.astype(BF16)

    for copy in small[1:]:
        copy.wait()
    place = iota((1, block_n), 1)
    row_of = jnp.zeros((1, block_n), jnp.int32)
    reach = jnp.zeros((1, block_n), jnp.int32)
    start = jnp.int32(0)
    for r in range(ROWS):
        end = start + counts_s[0, r]
        inside = (place >= start) & (place < end)
        row_of = jnp.where(inside, r, row_of)
        reach = jnp.where(inside, (end - 1) * BLOCK_TOKENS + tail_s[r], reach)
        start = end
    limit = jnp.clip(reach - place * BLOCK_TOKENS, 0, BLOCK_TOKENS)
    code = (row_of * 256 + limit).astype(F32)
    block_id = iota((block_n, block_n), 0)
    code_b = jnp.sum(jnp.where(order_v[...] == block_id, code, 0.0), axis=1, keepdims=True)
    lands = landing_v[...] == block_id
    table = jnp.sum(jnp.where(lands, code_b, 0.0), axis=0, keepdims=True)
    table_row = sum(jnp.where(table >= 256.0 * r, 1.0, 0.0) for r in range(1, ROWS))
    table_live = table - 256.0 * table_row

    routes = routes_v[...].reshape(1, route_n)
    entry = iota((1, route_n), 1)
    owner = ((entry.astype(F32) + 0.5) * (1.0 / fresh_n)).astype(jnp.int32)
    spot = entry - owner * fresh_n
    arrival = owner * CAPACITY
    for k in range(1, fresh_n):
        twin = (spot >= k) & (pltpu.roll(routes, k, 1) == routes)
        arrival = arrival + jnp.where(twin, 1, 0)
    arrival = jnp.where(routes == d, arrival, -1)
    comes = jnp.where(iota((block_n, route_n), 0) == arrival, 1.0, 0.0).astype(BF16)
    arrived = dot_nt(jnp.ones((8, route_n), BF16), comes)[0:1]
    replaced = jnp.sum(jnp.where(lands, arrived, 0.0), axis=1, keepdims=True)

    sub_b = iota((8, block_n), 0)
    sub_r = iota((8, route_n), 0)
    facts = jnp.where(
        sub_b == 0,
        table_row * 4.0 + (d * ROWS * OWN).astype(F32),
        jnp.where(sub_b == 1, table_live, 0.0),
    )
    facts = dot_nn(facts.astype(BF16), comes)
    facts = jnp.where(sub_r < 2, facts, 0.0)
    pad = jnp.zeros((8, HD - plane_n), F32)
    for g in range(dp_n):
        part = jnp.concatenate([facts[:, g * plane_n : (g + 1) * plane_n], pad], axis=1)
        tx0[g, 0:16, :] = q_own_v[...]
        tx0[g, 16:32, :] = jnp.concatenate([part, jnp.zeros((8, HD), F32)], axis=0).astype(BF16)

    slot_at = iota((block_n, HD), 1)
    slot_of = ((slot_at // 16) * tp_n + t) * CAPACITY + (slot_at % 16) // 8
    spread = jnp.where((iota((block_n, HD), 0) == slot_of) & (slot_at < 16 * dp_n), 1.0, 0.0)
    back_row = dot_nn(jnp.broadcast_to(table_row, (8, block_n)).astype(BF16), spread.astype(BF16))

    def a1(to):
        return pltpu.make_async_remote_copy(
            tx0.at[to], rx0.at[d], a1_send.at[to], a1_recv.at[d],
            device_id=(to, t), device_id_type=MESH,
        )

    def a1_from(come):
        return pltpu.make_async_remote_copy(
            tx0.at[come], rx0.at[come], a1_send.at[come], a1_recv.at[come],
            device_id=(come, t), device_id_type=MESH,
        )

    to_mate = pltpu.make_async_remote_copy(
        q_own_v, q_mate, mate_send, mate_recv, device_id=(d, mate), device_id_type=MESH
    )
    pl.semaphore_wait(barrier, dp_n + tp_n - 2)
    for to in dp_partners:
        a1(to).start()
    to_mate.start()
    rx0[d] = tx0[d]

    code_live = jnp.where(replaced > 0.0, 0.0, code_b)
    for r in range(ROWS):
        tokens = code_live - 256.0 * r
        tokens = jnp.where((tokens > 0.0) & (tokens <= float(BLOCK_TOKENS)), tokens, 0.0)
        tokens = jnp.clip(tokens - (half * HALF).astype(F32), 0.0, float(HALF))
        lim[r] = jnp.broadcast_to(2.0 * tokens, (block_n, HD))

    pick_n = 32 * tp_n
    pick_row = iota((pick_n, HD), 0)
    pick_at = pick_row % 32
    pick_from = jnp.where(
        (pick_at < fresh_n * OWN) & (iota((pick_n, HD), 1) == pick_row // 32 * fresh_n + pick_at // OWN),
        1.0,
        0.0,
    ).astype(BF16)
    pick_head = jnp.where(pick_at < fresh_n * OWN, iota((pick_n, HD), 1) - pick_at % OWN, -1)
    pick_head = pick_head.astype(F32)
    live_row = iota((8 * fresh_n, HD), 0) // 8
    live_from = jnp.where(iota((8 * fresh_n, HD), 1) == t * fresh_n + live_row, 1.0, 0.0).astype(BF16)

    each_dp(lambda come: a1_from(come).wait_recv())
    facts = rx0[0, 16:32, :].astype(F32)[0:8]
    for g in range(1, dp_n):
        facts = facts + rx0[g, 16:32, :].astype(F32)[0:8]
    index = jnp.broadcast_to(facts[0:1], (HD, HD)).astype(BF16)
    hot = jnp.where(dot_nt(pick_from, index) == pick_head, 1.0, 0.0).astype(BF16)
    tiles = jnp.concatenate([rx0[g, 0:16, :] for g in range(dp_n)], axis=0)
    picks[...] = dot_nn(hot[:, : 16 * dp_n], tiles).astype(BF16)

    def a2(to):
        return pltpu.make_async_remote_copy(
            picks.at[pl.ds(pl.multiple_of(to * 32, 32), 32)], rx1.at[t], a2_send.at[to], a2_recv.at[t],
            device_id=(d, to), device_id_type=MESH,
        )

    def a2_from(come):
        return pltpu.make_async_remote_copy(
            picks.at[pl.ds(pl.multiple_of(come * 32, 32), 32)], rx1.at[come], a2_send.at[come], a2_recv.at[come],
            device_id=(d, come), device_id_type=MESH,
        )

    for to in tp_partners:
        a2(to).start()
    rx1[t] = picks[pl.ds(pl.multiple_of(t * 32, 32), 32), :]
    live_tokens = jnp.broadcast_to(facts[1:2], (HD, HD)).astype(BF16)
    live_tokens = dot_nt(live_from, live_tokens)

    to_mate.wait_recv()
    q_other = q_mate[...].astype(F32)
    low = jnp.where(half == 0, q_own, q_other)
    high = jnp.where(half == 0, q_other, q_own)
    parts = []
    for r in range(ROWS):
        a = low[8 * (r // 2) : 8 * (r // 2) + 8]
        b = high[8 * (r // 2) : 8 * (r // 2) + 8]
        if r % 2 == 0:
            b = pltpu.roll(b, 4, 0)
        else:
            a = pltpu.roll(a, 4, 0)
        parts.append(jnp.where(sub < 4, a, b))
    q_pool = jnp.concatenate(parts, axis=0).astype(BF16)

    even_lane = jnp.where(lane % 2 == 0, lane, 1 << 20).astype(F32)

    def pool_scores(c, tops):
        pool_copy(c).wait()
        base = pl.multiple_of(c * rows_of_chunk, rows_of_chunk)
        s = dot_nt(q_pool, pool_v[pl.ds(base, rows_of_chunk), :])
        tops = list(tops)
        for j in range(POOL_CHUNK):
            for r in range(ROWS):
                bound = jnp.broadcast_to(lim[r, pl.ds(c * POOL_CHUNK + j, 1), :], (8, HD))
                piece = s[8 * r : 8 * r + 8, j * HD : (j + 1) * HD]
                piece = jnp.where(even_lane < bound, piece, NEG)
                tops[r] = jnp.maximum(tops[r], piece)
                scores[8 * r : 8 * r + 8, pl.ds(base + j * HD, HD)] = piece
        return tuple(tops)

    tops = lax.fori_loop(0, chunk_n, pool_scores, (jnp.full((8, HD), NEG, F32),) * ROWS)
    pool_top = [jnp.maximum(jnp.max(x, axis=1, keepdims=True), 0.1 * NEG) for x in tops]

    fresh_copy.wait()
    wide = iota((8, 2 * HD), 1)
    token = jnp.where(wide % 2 == 0, wide // 2, 1 << 20).astype(F32)
    each_tp(lambda come: a2_from(come).wait_recv())

    def unit(i, k):
        return (i * kv_n + k) * 2 * BLOCK_TOKENS

    for k in range(kv_n):
        sides = [rx1[2 * k + s].astype(F32) for s in range(2)]
        for i in range(fresh_n):
            a, b = (x[8 * (i // 2) : 8 * (i // 2) + 8] for x in sides)
            if i % 2 == 0:
                b = pltpu.roll(b, 4, 0)
            else:
                a = pltpu.roll(a, 4, 0)
            q_k = jnp.where(sub < 4, a, b).astype(BF16)
            at = unit(i, k)
            fscore[(i * kv_n + k) * 8 : (i * kv_n + k) * 8 + 8, :] = dot_nt(
                q_k, fresh_v[at : at + 2 * BLOCK_TOKENS, :]
            )
    kept = [jnp.zeros((8, HD), F32)] * kv_n
    for i in range(fresh_n):
        live = live_tokens[8 * i : 8 * i + 8]
        seen = token < jnp.concatenate([live, live], axis=1)
        for k in range(kv_n):
            at = (i * kv_n + k) * 8
            s = jnp.where(seen, fscore[at : at + 8, :], NEG)
            top = jnp.max(s, axis=1, keepdims=True)
            p = jnp.exp2((s - top) * FACTOR)
            total = jnp.sum(p, axis=1, keepdims=True)
            p = jnp.concatenate([pltpu.roll(p[:, :HD], 1, 1), pltpu.roll(p[:, HD:], 1, 1)], axis=1)
            fscore[at : at + 8, :] = p
            kept[k] = jnp.where(lane == i, top, kept[k])
            kept[k] = jnp.where(lane == 8 + i, total, kept[k])
    stat[...] = jnp.concatenate(kept + [jnp.zeros((HD - 8 * kv_n, HD), F32)], axis=0)
    for i in range(fresh_n):
        for k in range(kv_n):
            at = (i * kv_n + k) * 8
            facc[i, 8 * k : 8 * k + 8, :] = dot_nn(
                fscore[at : at + 8, :].astype(BF16),
                fresh_v[unit(i, k) : unit(i, k) + 2 * BLOCK_TOKENS, :],
            )
    stat_t[...] = jnp.transpose(stat[...])
    diagonal = (lane // 8) == sub
    for i in range(fresh_n):
        for at, keep in ((i, rows_top), (8 + i, rows_sum)):
            x = jnp.where(diagonal, jnp.broadcast_to(stat_t[at : at + 1, :], (8, HD)), 0.0)
            for shift in (8, 16, 32, 64):
                x = x + pltpu.roll(x, shift, 1)
            keep[i] = x

    first_own = source * fresh_n
    mine = [routes_s[first_own + i] for i in range(fresh_n)]
    ranks = []
    for i in range(fresh_n):
        rank = jnp.int32(0)
        for j in range(i):
            rank = rank + (mine[j] == mine[i]).astype(jnp.int32)
        ranks.append(rank)

    def c1(to):
        return pltpu.make_async_remote_copy(
            txc.at[to], rxc.at[d], c1_send.at[to], c1_recv.at[d],
            device_id=(to, t), device_id_type=MESH,
        )

    def c1_from(come):
        return pltpu.make_async_remote_copy(
            txc.at[come], rxc.at[come], c1_send.at[come], c1_recv.at[come],
            device_id=(come, t), device_id_type=MESH,
        )

    def pack(g):
        chosen, there = [], []
        for slot in range(CAPACITY):
            spot_at, hit = jnp.int32(0), jnp.int32(0)
            for i in range(fresh_n):
                ok = ((mine[i] == g) & (ranks[i] == slot)).astype(jnp.int32)
                spot_at = spot_at + ok * i
                hit = hit + ok
            chosen.append(spot_at)
            there.append(hit > 0)
        for k in range(kv_n):
            both = [
                jnp.where(there[s], facc[chosen[s], 8 * k : 8 * k + 8, :], 0.0)
                for s in range(CAPACITY)
            ]
            txc[g, 16 * k : 16 * k + 16, :] = jnp.concatenate(both, axis=0).astype(BF16)
        top = [jnp.where(there[s], rows_top[chosen[s]], NEG) for s in range(CAPACITY)]
        total = [jnp.where(there[s], rows_sum[chosen[s]], 0.0) for s in range(CAPACITY)]
        first = lane % 16 < 8
        top_1, rest = split(jnp.where(first, top[0], top[1]))
        top_2, top_3 = split(rest)
        total_1, total_2 = split(jnp.where(first, total[0], total[1]))
        x = jnp.where(lane < 16, top_1, jnp.where(lane < 32, top_2, top_3))
        x = jnp.where(lane < 48, x, jnp.where(lane < 64, total_1, total_2))
        x = jnp.where(lane < 80, x, 0.0)
        x = jnp.concatenate([x, jnp.zeros((8, HD), F32)], axis=0)
        txc[g, 16 * kv_n : 16 * kv_n + 16, :] = x.astype(BF16)

    for to in dp_partners:
        pack(to)
        c1(to).start()
    pack(d)
    rxc[d] = txc[d]

    def pool_values(c, carry):
        acc, sums = carry
        base = pl.multiple_of(c * rows_of_chunk, rows_of_chunk)
        sums = list(sums)
        columns = []
        for j in range(POOL_CHUNK):
            pieces = []
            for r in range(ROWS):
                piece = scores[8 * r : 8 * r + 8, pl.ds(base + j * HD, HD)]
                p = jnp.exp2((piece - pool_top[r]) * FACTOR)
                sums[r] = sums[r] + p
                pieces.append(pltpu.roll(p, 1, 1))
            columns.append(jnp.concatenate(pieces, axis=0).astype(BF16))
        p_all = jnp.concatenate(columns, axis=1)
        acc = acc + dot_nn(p_all, pool_v[pl.ds(base, rows_of_chunk), :])
        return acc, tuple(sums)

    pool_acc, sums = lax.fori_loop(
        0,
        chunk_n,
        pool_values,
        (jnp.zeros((8 * ROWS, HD), F32), (jnp.zeros((8, HD), F32),) * ROWS),
    )
    pool_sum = [jnp.sum(x, axis=1, keepdims=True) for x in sums]

    each_dp(lambda come: c1_from(come).wait_recv())
    all_tops = jnp.zeros((8, HD), F32)
    all_sums = jnp.zeros((8, HD), F32)
    for g in range(dp_n):
        x = rxc[g, 16 * kv_n : 16 * kv_n + 16, :].astype(F32)[0:8]
        top = (x + pltpu.roll(x, HD - 16, 1)) + pltpu.roll(x, HD - 32, 1)
        total = pltpu.roll(x, HD - 48, 1) + pltpu.roll(x, HD - 64, 1)
        if g:
            top = pltpu.roll(top, 16 * g, 1)
            total = pltpu.roll(total, 16 * g, 1)
        here = (lane >= 16 * g) & (lane < 16 * g + 16)
        all_tops = jnp.where(here, top, all_tops)
        all_sums = jnp.where(here, total, all_sums)
    of_head = (lane % 8 == sub) & (lane < 16 * dp_n)
    of_rows = [of_head & (back_row == float(r)) for r in range(ROWS)]

    def c2(to):
        return pltpu.make_async_remote_copy(
            tx2.at[to], rx2.at[t], c2_send.at[to], c2_recv.at[t],
            device_id=(d, to), device_id_type=MESH,
        )

    def c2_from(come):
        return pltpu.make_async_remote_copy(
            tx2.at[come], rx2.at[come], c2_send.at[come], c2_recv.at[come],
            device_id=(d, come), device_id_type=MESH,
        )

    for m in range(kv_n):
        tops_in = jnp.broadcast_to(all_tops[m : m + 1], (8, HD))
        sums_in = jnp.broadcast_to(all_sums[m : m + 1], (8, HD))
        here = kv == m
        best, masses, weights, pool_weights = [], [], [], []
        for r in range(ROWS):
            top = jnp.max(jnp.where(of_rows[r], tops_in, NEG), axis=1, keepdims=True)
            top = jnp.maximum(top, jnp.where(here, pool_top[r], NEG))
            w = jnp.where(of_rows[r], jnp.exp2((tops_in - top) * FACTOR), 0.0)
            w_pool = jnp.where(here, jnp.exp2((pool_top[r] - top) * FACTOR), 0.0)
            masses.append(jnp.sum(w * sums_in, axis=1, keepdims=True) + w_pool * pool_sum[r])
            best.append(top)
            weights.append(w)
            pool_weights.append(w_pool)
        w_1, w_2 = split(jnp.concatenate(weights, axis=0))
        x = jnp.concatenate([rxc[g, 16 * m : 16 * m + 16, :] for g in range(dp_n)], axis=0)
        w_1, w_2 = (v[:, : 16 * dp_n].astype(BF16) for v in (w_1, w_2))
        acc = dot_nn(w_1, x) + dot_nn(w_2, x)
        accs = [
            acc[8 * r : 8 * r + 8] + pool_weights[r] * pool_acc[8 * r : 8 * r + 8]
            for r in range(ROWS)
        ]
        def halves(v):
            low_half, high_half = [], []
            for pair in range(2):
                a, b = v[2 * pair], v[2 * pair + 1]
                low_half.append(jnp.where(sub < 4, a, pltpu.roll(b, 4, 0)))
                high_half.append(jnp.where(sub < 4, pltpu.roll(a, 4, 0), b))
            return low_half, high_half

        acc_halves = halves(accs)
        stat_halves = halves([jnp.where(lane % 64 < 32, best[r], masses[r]) for r in range(ROWS)])
        for s in range(2):
            to = 2 * m + s
            tx2[to, 0:8, :] = acc_halves[s][0]
            tx2[to, 8:16, :] = acc_halves[s][1]
            tx2[to, 16:24, :] = jnp.where(lane < 64, stat_halves[s][0], stat_halves[s][1])

            @pl.when(t != to)
            def _():
                c2(to).start()

    rx2[t] = tx2[t]

    new_kv_f[...] = new_kv_v[...].astype(F32)
    keys, values = [], []
    for r in range(ROWS):
        at = (r * kv_n + kv) * 2
        keys.append(jnp.broadcast_to(new_kv_f[pl.ds(at, 1), :], (OWN, HD)))
        values.append(jnp.broadcast_to(new_kv_f[pl.ds(at + 1, 1), :], (OWN, HD)))
    key_new = jnp.concatenate(keys, axis=0)
    value_new = jnp.concatenate(values, axis=0)
    score_new = jnp.sum(q_own * key_new, axis=1, keepdims=True)
    gains = jnp.concatenate(
        [
            jnp.concatenate(
                [
                    jnp.broadcast_to(gain_v[pl.ds(t * (share // HD) + s * (side // HD) + c, 1), :], (4, HD))
                    for s in range(2)
                ],
                axis=0,
            )
            for c in range(side // HD)
        ],
        axis=1,
    )
    res = jnp.concatenate([residual_v[:, :side], residual_v[:, side:]], axis=0).astype(F32)

    each_tp(lambda come: c2_from(come).wait_recv())
    new_low = jnp.broadcast_to(score_new[0:8], (8, HD))
    new_high = jnp.broadcast_to(score_new[8:16], (8, HD))
    top = jnp.where(lane < 64, new_low, new_high)
    for j in range(tp_n):
        top = jnp.maximum(top, rx2[j, 16:24, :])
    top = jnp.where(lane % 64 < 32, top, pltpu.roll(top, 32, 1))
    score = jnp.where(lane < 64, new_low, new_high)
    weight = jnp.exp2((score - top) * FACTOR)
    mass = weight

    def wide_rows(v):
        other = pltpu.roll(v, 64, 1)
        return jnp.where(lane < 64, v, other), jnp.where(lane < 64, other, v)

    acc = [w * value_new[8 * s : 8 * s + 8] for s, w in enumerate(wide_rows(weight))]
    for j in range(tp_n):
        their = rx2[j, 16:24, :]
        w = jnp.exp2((jnp.where(lane % 64 < 32, their, pltpu.roll(their, 32, 1)) - top) * FACTOR)
        mass = mass + w * their
        for s, v in enumerate(wide_rows(w)):
            acc[s] = acc[s] + v * rx2[j, 8 * s : 8 * s + 8, :]
    mass = jnp.where(lane % 64 < 32, pltpu.roll(mass, HD - 32, 1), mass)
    attended = [acc[s] / v for s, v in enumerate(wide_rows(mass))]

    qf[...] = jnp.concatenate(attended, axis=0)
    zeros = jnp.zeros((ROWS, OWN * HD), F32)
    flat = jnp.concatenate([qf[pl.ds(h, ROWS, stride=OWN), :] for h in range(OWN)], axis=1)
    first_rows = jnp.concatenate([flat, zeros], axis=0).astype(BF16)
    last_rows = jnp.concatenate([zeros, flat], axis=0).astype(BF16)
    w_copy.wait()

    def d_copy(to):
        return pltpu.make_async_remote_copy(
            tx3.at[to], rx3.at[t], d_send.at[to], d_recv.at[t],
            device_id=(d, to), device_id_type=MESH,
        )

    def d_from(come):
        return pltpu.make_async_remote_copy(
            tx3.at[come], rx3.at[come], d_send.at[come], d_recv.at[come],
            device_id=(d, come), device_id_type=MESH,
        )

    def project(to):
        base = pl.multiple_of(to * share, share)
        return dot_nn(first_rows, w_v[:, pl.ds(base, side)]) + dot_nn(
            last_rows, w_v[:, pl.ds(base + side, side)]
        )

    for to in tp_partners:
        tx3[to] = project(to)
        d_copy(to).start()
    rx3[t] = res + project(t)
    each_tp(lambda come: d_from(come).wait_recv())
    hidden = rx3[0]
    for j in range(1, tp_n):
        hidden = hidden + rx3[j]

    square = jnp.sum(hidden * hidden, axis=1, keepdims=True)
    square = jnp.broadcast_to(square, (8, HD))
    tx4[...] = square + pltpu.roll(square, 4, 0)

    def e_copy(to):
        return pltpu.make_async_remote_copy(
            tx4, rx4.at[t], e_send.at[to], e_recv.at[t],
            device_id=(d, to), device_id_type=MESH,
        )

    def e_from(come):
        return pltpu.make_async_remote_copy(
            tx4, rx4.at[come], e_send.at[come], e_recv.at[come],
            device_id=(d, come), device_id_type=MESH,
        )

    for to in tp_partners:
        e_copy(to).start()
    rx4[t] = tx4[...]
    to_mate.wait_send()
    each_dp(lambda to: a1(to).wait_send())
    each_tp(lambda to: a2(to).wait_send())
    each_dp(lambda to: c1(to).wait_send())
    each_tp(lambda to: c2(to).wait_send())
    each_tp(lambda to: d_copy(to).wait_send())
    each_tp(lambda come: e_from(come).wait_recv())
    square = rx4[0]
    for j in range(1, tp_n):
        square = square + rx4[j]
    scale = lax.rsqrt(square * (1.0 / width) + 1e-5)
    normed = hidden * jnp.concatenate([scale] * (side // HD), axis=1) * gains
    out_ref[...] = jnp.concatenate([normed[0:ROWS], normed[ROWS:]], axis=1).astype(BF16)
    each_tp(lambda to: e_copy(to).wait_send())


def local(
    dp_n, tp_n,
    pool, fresh_kv, routes, landing_order, pool_order, block_counts, tail_fill,
    queries, new_kv, w_out, residual, gain,
):
    block_n = pool.shape[0]
    fresh_n = fresh_kv.shape[0]
    kv_n = new_kv.shape[1]
    head_n = OWN * tp_n
    share = w_out.shape[1] // tp_n
    pool_rows = pool.reshape(block_n * BLOCK_TOKENS, HD)
    fresh_rows = fresh_kv.reshape(fresh_n * 2 * kv_n * BLOCK_TOKENS, HD)
    hbm = pl.BlockSpec(memory_space=pltpu.HBM)
    dma = pltpu.SemaphoreType.DMA
    message = 16 * kv_n + 16
    return pl.pallas_call(
        functools.partial(kernel, dp_n, tp_n, fresh_n, block_n),
        out_shape=jax.ShapeDtypeStruct((ROWS, share), BF16),
        in_specs=[hbm] * 12,
        out_specs=pl.BlockSpec(memory_space=pltpu.VMEM),
        scratch_shapes=[
            pltpu.SMEM(routes.shape, jnp.int32),
            pltpu.SMEM(block_counts.shape, jnp.int32),
            pltpu.SMEM(tail_fill.shape, jnp.int32),
            pltpu.VMEM(routes.shape, jnp.int32),
            pltpu.VMEM(landing_order.shape, jnp.int32),
            pltpu.VMEM(pool_order.shape, jnp.int32),
            pltpu.VMEM(queries.shape, BF16),
            pltpu.VMEM((ROWS * kv_n * 2, HD), BF16),
            pltpu.VMEM((ROWS, share), BF16),
            pltpu.VMEM((gain.shape[0] // HD, HD), F32),
            pltpu.VMEM(pool_rows.shape, BF16),
            pltpu.VMEM(fresh_rows.shape, BF16),
            pltpu.VMEM(w_out.shape, BF16),
            pltpu.VMEM((8 * ROWS, block_n * BLOCK_TOKENS), F32),
            pltpu.VMEM((ROWS, block_n, HD), F32),
            pltpu.VMEM((ROWS * OWN, HD), F32),
            pltpu.VMEM((ROWS * OWN, HD), BF16),
            pltpu.VMEM((ROWS * OWN, HD), BF16),
            pltpu.VMEM((ROWS * kv_n * 2, HD), F32),
            pltpu.VMEM((dp_n, 32, HD), BF16),
            pltpu.VMEM((dp_n, 32, HD), BF16),
            pltpu.VMEM((32 * tp_n, HD), BF16),
            pltpu.VMEM((tp_n, 32, HD), BF16),
            pltpu.VMEM((fresh_n * head_n, 2 * HD), F32),
            pltpu.VMEM((fresh_n, head_n, HD), F32),
            pltpu.VMEM((HD, HD), F32),
            pltpu.VMEM((HD, HD), F32),
            pltpu.VMEM((fresh_n, 8, HD), F32),
            pltpu.VMEM((fresh_n, 8, HD), F32),
            pltpu.VMEM((dp_n, message, HD), BF16),
            pltpu.VMEM((dp_n, message, HD), BF16),
            pltpu.VMEM((tp_n, 24, HD), F32),
            pltpu.VMEM((tp_n, 24, HD), F32),
            pltpu.VMEM((tp_n, 8, share // 2), F32),
            pltpu.VMEM((tp_n, 8, share // 2), F32),
            pltpu.VMEM((8, HD), F32),
            pltpu.VMEM((tp_n, 8, HD), F32),
            dma((10,)),
            dma((block_n // POOL_CHUNK,)),
            dma(()),
            dma(()),
            dma(()),
            dma(()),
            *[dma((dp_n,))] * 2,
            *[dma((tp_n,))] * 2,
            *[dma((dp_n,))] * 2,
            *[dma((tp_n,))] * 6,
        ],
        compiler_params=pltpu.CompilerParams(
            collective_id=0, has_side_effects=True, vmem_limit_bytes=56 << 20
        ),
    )(
        pool_rows,
        fresh_rows,
        w_out,
        routes,
        block_counts,
        tail_fill,
        landing_order,
        pool_order,
        queries,
        new_kv.reshape(-1, HD),
        residual,
        gain.reshape(-1, HD),
    )


def solution(mesh):
    return jax.shard_map(
        functools.partial(local, mesh.shape["dp"], mesh.shape["tensor"]),
        mesh=mesh,
        in_specs=(
            P("dp", "tensor", None, None, None),
            P(("dp", "tensor"), None, None, None, None),
            P(),
            P("dp", None),
            P("dp", None),
            P("dp", None),
            P("dp"),
            P("dp", "tensor"),
            P("dp", None, None, None),
            P("tensor", None),
            P("dp", None),
            P(),
        ),
        out_specs=P("dp", "tensor"),
        check_vma=False,
    )
```

time: 75.7 us -> 46.4 us (0.61)
  Pallas kernels: 65.7 us -> 45 us
  local copies, waits for them, and re-layouts: 8.94 us -> 1.28 us
    pallas_call x1, Pallas kernels: 65.7 us -> 45 us  [local(): pl.pallas_call(functools.partial(kernel, dp_n, tp_n, fresh_n, block_n), o...]
    unnamed x18 -> x1, local copies, waits for them, and re-layouts: 7.48 us -> 1.28 us
    dynamic_slice x1 -> x0, local copies, waits for them, and re-layouts: 0.76 us -> none  [local(): gains = lax.dynamic_slice_in_dim(gain, spot, share, 0)]
where the time goes in v2:
time: 46.4 us; the launch traced here: 46.3 us
  Pallas kernels  45 us (97%)
  local copies, waits for them, and re-layouts  1.28 us (3%)
    pallas_call x1, Pallas kernels, local(): pl.pallas_call(functools.partial(kernel, dp_n, tp_n, fresh_n, block_n), o...  45 us
    unnamed x1, local copies, waits for them, and re-layouts  1.28 us

profile of v2, /device:TPU:0, one launch (start us, length us, event | category | flops | bytes accessed | tf_op | source)
XLA Modules:
  0.0 46.3 jit_solution(11670458881189115292)
XLA Ops:
  0.0 45.0 %shard_map.118 = bf16[4,512]{1,0:T(4,128)(2,1)} custom-call(bf16[32768,128]{1,0:T(8,128)(2,1)} %bitcast.4, bf16[12288,128]{1,0:T(8,128)(2,1)} %bitcast.5, bf16[512,8192]{1,0:T(8,128)(2,1)} %w_hbm.1, s32[768]{0:T(1024)} %routes_hbm.1, s32[1,4]{1,0:T(1,128)} %counts_hbm.1, s32[4]{0:T(128)} %tail_hbm.1, s32[1,256]{1,0:T(1,128)} %landing_hbm.1, ...), custom_call_target="tpu_custom_call" | custom-call | tf_op jit(solution)/shard_map/pallas_call | solution.py:633
  45.0 1.3 %copy.14 = bf16[4,512]{1,0:T(4,128)(2,1)} copy(bf16[4,512]{1,0:T(4,128)(2,1)} %shard_map.118) | data formatting | bytes 8192

commit v3 on v2

--- a/solution.py
+++ b/solution.py
@@ -17,7 +17,7 @@
 CAPACITY = 2
 NEG = -1e30
 FACTOR = math.log2(math.e) / math.sqrt(HD)
-POOL_CHUNK = 16
+POOL_CHUNK = 64
 F32, BF16 = jnp.float32, jnp.bfloat16
 
 
@@ -126,8 +126,6 @@
     fresh_copy = pltpu.make_async_copy(fresh_hbm, fresh_v, fresh_sem)
     w_copy = pltpu.make_async_copy(w_hbm, w_v, w_sem)
     loop(0, chunk_n, lambda c: pool_copy(c).start())
-    fresh_copy.start()
-    w_copy.start()
 
     sub = iota((8, HD), 0)
     lane = iota((8, HD), 1)
@@ -210,6 +208,8 @@
     for to in dp_partners:
         a1(to).start()
     to_mate.start()
+    fresh_copy.start()
+    w_copy.start()
     rx0[d] = tx0[d]
 
     code_live = jnp.where(replaced > 0.0, 0.0, code_b)
@@ -491,10 +491,8 @@
             tx2[to, 8:16, :] = acc_halves[s][1]
             tx2[to, 16:24, :] = jnp.where(lane < 64, stat_halves[s][0], stat_halves[s][1])
 
-            @pl.when(t != to)
-            def _():
-                c2(to).start()
-
+    for to in tp_partners:
+        c2(to).start()
     rx2[t] = tx2[t]
 
     new_kv_f[...] = new_kv_v[...].astype(F32)
@@ -571,9 +569,11 @@
             last_rows, w_v[:, pl.ds(base + side, side)]
         )
 
-    for to in tp_partners:
-        tx3[to] = project(to)
-        d_copy(to).start()
+    for at in range(0, tp_n - 1, 5):
+        for to in tp_partners[at : at + 5]:
+            tx3[to] = project(to)
+        for to in tp_partners[at : at + 5]:
+            d_copy(to).start()
     rx3[t] = res + project(t)
     each_tp(lambda come: d_from(come).wait_recv())
     hidden = rx3[0]

time: 46.4 us -> 43.1 us (0.929)
  Pallas kernels: 45 us -> 41.7 us
    pallas_call x1, Pallas kernels: 45 us -> 41.7 us  [local(): pl.pallas_call(functools.partial(kernel, dp_n, tp_n, fresh_n, block_n), o...]
where the time goes in v3:
time: 43.1 us; the launch traced here: 42.9 us
  Pallas kernels  41.7 us (97%)
  local copies, waits for them, and re-layouts  1.28 us (3%)
    pallas_call x1, Pallas kernels, local(): pl.pallas_call(functools.partial(kernel, dp_n, tp_n, fresh_n, block_n), o...  41.7 us
    unnamed x1, local copies, waits for them, and re-layouts  1.28 us

profile of v3, /device:TPU:0, one launch (start us, length us, event | category | flops | bytes accessed | tf_op | source)
XLA Modules:
  0.0 42.9 jit_solution(6677039422924683401)
XLA Ops:
  0.0 41.7 %shard_map.118 = bf16[4,512]{1,0:T(4,128)(2,1)} custom-call(bf16[32768,128]{1,0:T(8,128)(2,1)} %bitcast.4, bf16[12288,128]{1,0:T(8,128)(2,1)} %bitcast.5, bf16[512,8192]{1,0:T(8,128)(2,1)} %w_hbm.1, s32[768]{0:T(1024)} %routes_hbm.1, s32[1,4]{1,0:T(1,128)} %counts_hbm.1, s32[4]{0:T(128)} %tail_hbm.1, s32[1,256]{1,0:T(1,128)} %landing_hbm.1, ...), custom_call_target="tpu_custom_call" | custom-call | tf_op jit(solution)/shard_map/pallas_call | solution.py:633
  41.7 1.3 %copy.14 = bf16[4,512]{1,0:T(4,128)(2,1)} copy(bf16[4,512]{1,0:T(4,128)(2,1)} %shard_map.118) | data formatting | bytes 8192

commit v4 on v3

--- a/solution.py
+++ b/solution.py
@@ -43,17 +43,16 @@
     pool_hbm, fresh_hbm, w_hbm, routes_hbm, counts_hbm, tail_hbm, landing_hbm, order_hbm,
     queries_hbm, new_kv_hbm, residual_hbm, gain_hbm,
     out_ref,
-    routes_s, counts_s, tail_s, routes_v, landing_v, order_v, queries_v, new_kv_v, residual_v, gain_v,
+    counts_s, tail_s, routes_v, landing_v, order_v, queries_v, new_kv_v, residual_v, gain_v,
     pool_v, fresh_v, w_v, scores, lim, qf, q_own_v, q_mate, new_kv_f,
-    tx0, rx0, picks, rx1, fscore, facc, stat, stat_t, rows_top, rows_sum,
-    txc, rxc, tx2, rx2, tx3, rx3, tx4, rx4,
+    tx0, rx0, picks, rx1, fscore, facc, stat, stat_t,
+    txc, rxc, tx_pool, shares, tx2, rx2, tx3, rx3, tx4, rx4,
     small_sem, pool_sem, fresh_sem, w_sem,
-    mate_send, mate_recv, a1_send, a1_recv, a2_send, a2_recv,
+    mate_send, mate_recv, pool_send, pool_recv, a1_send, a1_recv, a2_send, a2_recv,
     c1_send, c1_recv, c2_send, c2_recv, d_send, d_recv, e_send, e_recv,
 ):
     d = lax.axis_index("dp")
     t = lax.axis_index("tensor")
-    source = d * tp_n + t
     kv_n = tp_n // 2
     kv = t // 2
     half = t % 2
@@ -96,6 +95,12 @@
     def each_tp(act):
         loop(1, tp_n, lambda j: act(lax.rem(t + j, tp_n)))
 
+    barrier = pltpu.get_barrier_semaphore()
+    for to in tp_partners:
+        pl.semaphore_signal(barrier, 1, device_id=(d, to), device_id_type=MESH)
+    for to in dp_partners:
+        pl.semaphore_signal(barrier, 1, device_id=(to, t), device_id_type=MESH)
+
     at_share = pl.ds(pl.multiple_of(t * share, share), share)
     small = [
         (queries_hbm, queries_v),
@@ -104,7 +109,6 @@
         (order_hbm, order_v),
         (counts_hbm, counts_s),
         (tail_hbm, tail_s),
-        (routes_hbm, routes_s),
         (new_kv_hbm, new_kv_v),
         (residual_hbm.at[:, at_share], residual_v),
         (gain_hbm, gain_v),
@@ -112,12 +116,6 @@
     small = [pltpu.make_async_copy(a, b, small_sem.at[i]) for i, (a, b) in enumerate(small)]
     for copy in small:
         copy.start()
-
-    barrier = pltpu.get_barrier_semaphore()
-    for to in tp_partners:
-        pl.semaphore_signal(barrier, 1, device_id=(d, to), device_id_type=MESH)
-    for to in dp_partners:
-        pl.semaphore_signal(barrier, 1, device_id=(to, t), device_id_type=MESH)
 
     def pool_copy(c):
         at = pl.ds(pl.multiple_of(c * rows_of_chunk, rows_of_chunk), rows_of_chunk)
@@ -166,8 +164,6 @@
         arrival = arrival + jnp.where(twin, 1, 0)
     arrival = jnp.where(routes == d, arrival, -1)
     comes = jnp.where(iota((block_n, route_n), 0) == arrival, 1.0, 0.0).astype(BF16)
-    arrived = dot_nt(jnp.ones((8, route_n), BF16), comes)[0:1]
-    replaced = jnp.sum(jnp.where(lands, arrived, 0.0), axis=1, keepdims=True)
 
     sub_b = iota((8, block_n), 0)
     sub_r = iota((8, route_n), 0)
@@ -184,11 +180,6 @@
         tx0[g, 0:16, :] = q_own_v[...]
         tx0[g, 16:32, :] = jnp.concatenate([part, jnp.zeros((8, HD), F32)], axis=0).astype(BF16)
 
-    slot_at = iota((block_n, HD), 1)
-    slot_of = ((slot_at // 16) * tp_n + t) * CAPACITY + (slot_at % 16) // 8
-    spread = jnp.where((iota((block_n, HD), 0) == slot_of) & (slot_at < 16 * dp_n), 1.0, 0.0)
-    back_row = dot_nn(jnp.broadcast_to(table_row, (8, block_n)).astype(BF16), spread.astype(BF16))
-
     def a1(to):
         return pltpu.make_async_remote_copy(
             tx0.at[to], rx0.at[d], a1_send.at[to], a1_recv.at[d],
@@ -211,6 +202,9 @@
     fresh_copy.start()
     w_copy.start()
     rx0[d] = tx0[d]
+
+    arrived = dot_nt(jnp.ones((8, route_n), BF16), comes)[0:1]
+    replaced = jnp.sum(jnp.where(lands, arrived, 0.0), axis=1, keepdims=True)
 
     code_live = jnp.where(replaced > 0.0, 0.0, code_b)
     for r in range(ROWS):
@@ -258,6 +252,14 @@
     rx1[t] = picks[pl.ds(pl.multiple_of(t * 32, 32), 32), :]
     live_tokens = jnp.broadcast_to(facts[1:2], (HD, HD)).astype(BF16)
     live_tokens = dot_nt(live_from, live_tokens)
+
+    pick_lane = iota((dp_n * ROWS * OWN, pick_n), 1)
+    pick_spot = pick_lane % 32
+    pick_place = jnp.where(
+        pick_spot < fresh_n * OWN, iota(pick_lane.shape, 0) - pick_spot % OWN, -1
+    ).astype(F32)
+    index_row = dot_nt(index[0:8], pick_from)
+    hot_row = jnp.broadcast_to(index_row[0:1], pick_lane.shape) == pick_place
 
     to_mate.wait_recv()
     q_other = q_mate[...].astype(F32)
@@ -337,68 +339,56 @@
                 fresh_v[unit(i, k) : unit(i, k) + 2 * BLOCK_TOKENS, :],
             )
     stat_t[...] = jnp.transpose(stat[...])
-    diagonal = (lane // 8) == sub
-    for i in range(fresh_n):
-        for at, keep in ((i, rows_top), (8 + i, rows_sum)):
-            x = jnp.where(diagonal, jnp.broadcast_to(stat_t[at : at + 1, :], (8, HD)), 0.0)
-            for shift in (8, 16, 32, 64):
-                x = x + pltpu.roll(x, shift, 1)
-            keep[i] = x
-
-    first_own = source * fresh_n
-    mine = [routes_s[first_own + i] for i in range(fresh_n)]
-    ranks = []
-    for i in range(fresh_n):
-        rank = jnp.int32(0)
-        for j in range(i):
-            rank = rank + (mine[j] == mine[i]).astype(jnp.int32)
-        ranks.append(rank)
+    own_lanes = (lane // OWN == sub) & (sub < fresh_n)
+
+    def shifted(x):
+        return jnp.concatenate(
+            [pltpu.roll(x[i : i + 1], OWN * i, 1) if i else x[0:1] for i in range(8)], axis=0
+        )
+
+    tops_of, sums_of = shifted(stat_t[0:8, :]), shifted(stat_t[8:16, :])
+
+    def row_for(x, to):
+        x = pltpu.roll(x, HD - OWN * to, 1) if to else x
+        x = jnp.sum(jnp.where(own_lanes, x, 0.0), axis=0, keepdims=True)
+        return jnp.broadcast_to(x, (8, HD))
+
+    def halves(v):
+        low_half, high_half = [], []
+        for a, b in zip(v[0::2], v[1::2]):
+            low_half.append(jnp.where(sub < 4, a, pltpu.roll(b, 4, 0)))
+            high_half.append(jnp.where(sub < 4, pltpu.roll(a, 4, 0), b))
+        return low_half, high_half
+
+    for k in range(kv_n):
+        tiles_of = halves([facc[i, 8 * k : 8 * k + 8, :] for i in range(fresh_n)])
+        for s in range(2):
+            to = 2 * k + s
+            top_1, rest = split(row_for(tops_of, to))
+            top_2, top_3 = split(rest)
+            sum_1, sum_2 = split(row_for(sums_of, to))
+            x = jnp.where(sub == 0, top_1, jnp.where(sub == 1, top_2, top_3))
+            x = jnp.where(sub < 3, x, jnp.where(sub == 3, sum_1, sum_2))
+            x = jnp.where((sub < 5) & (lane < fresh_n * OWN), x, 0.0)
+            x = pltpu.roll(x, lax.rem(t, 4) * 32, 1)
+            gap = [jnp.zeros((8, HD), F32)] * (3 - len(tiles_of[s]))
+            txc[to] = jnp.concatenate(tiles_of[s] + gap + [x], axis=0).astype(BF16)
 
     def c1(to):
         return pltpu.make_async_remote_copy(
-            txc.at[to], rxc.at[d], c1_send.at[to], c1_recv.at[d],
-            device_id=(to, t), device_id_type=MESH,
+            txc.at[to], rxc.at[t], c1_send.at[to], c1_recv.at[t],
+            device_id=(d, to), device_id_type=MESH,
         )
 
     def c1_from(come):
         return pltpu.make_async_remote_copy(
             txc.at[come], rxc.at[come], c1_send.at[come], c1_recv.at[come],
-            device_id=(come, t), device_id_type=MESH,
-        )
-
-    def pack(g):
-        chosen, there = [], []
-        for slot in range(CAPACITY):
-            spot_at, hit = jnp.int32(0), jnp.int32(0)
-            for i in range(fresh_n):
-                ok = ((mine[i] == g) & (ranks[i] == slot)).astype(jnp.int32)
-                spot_at = spot_at + ok * i
-                hit = hit + ok
-            chosen.append(spot_at)
-            there.append(hit > 0)
-        for k in range(kv_n):
-            both = [
-                jnp.where(there[s], facc[chosen[s], 8 * k : 8 * k + 8, :], 0.0)
-                for s in range(CAPACITY)
-            ]
-            txc[g, 16 * k : 16 * k + 16, :] = jnp.concatenate(both, axis=0).astype(BF16)
-        top = [jnp.where(there[s], rows_top[chosen[s]], NEG) for s in range(CAPACITY)]
-        total = [jnp.where(there[s], rows_sum[chosen[s]], 0.0) for s in range(CAPACITY)]
-        first = lane % 16 < 8
-        top_1, rest = split(jnp.where(first, top[0], top[1]))
-        top_2, top_3 = split(rest)
-        total_1, total_2 = split(jnp.where(first, total[0], total[1]))
-        x = jnp.where(lane < 16, top_1, jnp.where(lane < 32, top_2, top_3))
-        x = jnp.where(lane < 48, x, jnp.where(lane < 64, total_1, total_2))
-        x = jnp.where(lane < 80, x, 0.0)
-        x = jnp.concatenate([x, jnp.zeros((8, HD), F32)], axis=0)
-        txc[g, 16 * kv_n : 16 * kv_n + 16, :] = x.astype(BF16)
-
-    for to in dp_partners:
-        pack(to)
+            device_id=(d, come), device_id_type=MESH,
+        )
+
+    for to in tp_partners:
         c1(to).start()
-    pack(d)
-    rxc[d] = txc[d]
+    rxc[t] = txc[t]
 
     def pool_values(c, carry):
         acc, sums = carry
@@ -425,75 +415,60 @@
     )
     pool_sum = [jnp.sum(x, axis=1, keepdims=True) for x in sums]
 
-    each_dp(lambda come: c1_from(come).wait_recv())
-    all_tops = jnp.zeros((8, HD), F32)
-    all_sums = jnp.zeros((8, HD), F32)
+    def share_tile(acc, top, total):
+        stats = [jnp.where(lane % 64 < 32, a, b) for a, b in zip(top, total)]
+        return acc + [jnp.where(lane < 64, stats[0], stats[1])]
+
+    pool_halves = halves([pool_acc[8 * r : 8 * r + 8] for r in range(ROWS)])
+    top_halves = halves([jnp.broadcast_to(x, (8, HD)) for x in pool_top])
+    sum_halves = halves([jnp.broadcast_to(x, (8, HD)) for x in pool_sum])
+    low_tile, high_tile = (
+        jnp.concatenate(share_tile(pool_halves[s], top_halves[s], sum_halves[s]), axis=0)
+        for s in range(2)
+    )
+    shares[0] = jnp.where(half == 0, low_tile, high_tile)
+    tx_pool[...] = jnp.where(half == 0, high_tile, low_tile)
+    pool_to_mate = pltpu.make_async_remote_copy(
+        tx_pool, shares.at[1], pool_send, pool_recv, device_id=(d, mate), device_id_type=MESH
+    )
+    pool_to_mate.start()
+
+    each_tp(lambda come: c1_from(come).wait_recv())
+    tops_in, sums_in = [], []
+    for q in range(tp_n // 4):
+        x = rxc[4 * q].astype(F32)[24:32]
+        for s in range(1, 4):
+            x = x + rxc[4 * q + s].astype(F32)[24:32]
+        tops_in.append((x[0:1] + x[1:2]) + x[2:3])
+        sums_in.append(x[3:4] + x[4:5])
+    tops_in = jnp.broadcast_to(jnp.concatenate(tops_in, axis=1), pick_lane.shape)
+    sums_in = jnp.broadcast_to(jnp.concatenate(sums_in, axis=1), pick_lane.shape)
+    best = jnp.max(jnp.where(hot_row, tops_in, NEG), axis=1, keepdims=True)
+    weight = jnp.where(hot_row, jnp.exp2((tops_in - best) * FACTOR), 0.0)
+    mass = jnp.sum(weight * sums_in, axis=1, keepdims=True)
+    w_1, w_2 = split(weight)
+    x = rxc[...].reshape(pick_n, HD)
+    acc = dot_nn(w_1.astype(BF16), x) + dot_nn(w_2.astype(BF16), x)
+
+    def c2(to):
+        return pltpu.make_async_remote_copy(
+            tx2.at[to], rx2.at[d], c2_send.at[to], c2_recv.at[d],
+            device_id=(to, t), device_id_type=MESH,
+        )
+
+    def c2_from(come):
+        return pltpu.make_async_remote_copy(
+            tx2.at[come], rx2.at[come], c2_send.at[come], c2_recv.at[come],
+            device_id=(come, t), device_id_type=MESH,
+        )
+
     for g in range(dp_n):
-        x = rxc[g, 16 * kv_n : 16 * kv_n + 16, :].astype(F32)[0:8]
-        top = (x + pltpu.roll(x, HD - 16, 1)) + pltpu.roll(x, HD - 32, 1)
-        total = pltpu.roll(x, HD - 48, 1) + pltpu.roll(x, HD - 64, 1)
-        if g:
-            top = pltpu.roll(top, 16 * g, 1)
-            total = pltpu.roll(total, 16 * g, 1)
-        here = (lane >= 16 * g) & (lane < 16 * g + 16)
-        all_tops = jnp.where(here, top, all_tops)
-        all_sums = jnp.where(here, total, all_sums)
-    of_head = (lane % 8 == sub) & (lane < 16 * dp_n)
-    of_rows = [of_head & (back_row == float(r)) for r in range(ROWS)]
-
-    def c2(to):
-        return pltpu.make_async_remote_copy(
-            tx2.at[to], rx2.at[t], c2_send.at[to], c2_recv.at[t],
-            device_id=(d, to), device_id_type=MESH,
-        )
-
-    def c2_from(come):
-        return pltpu.make_async_remote_copy(
-            tx2.at[come], rx2.at[come], c2_send.at[come], c2_recv.at[come],
-            device_id=(d, come), device_id_type=MESH,
-        )
-
-    for m in range(kv_n):
-        tops_in = jnp.broadcast_to(all_tops[m : m + 1], (8, HD))
-        sums_in = jnp.broadcast_to(all_sums[m : m + 1], (8, HD))
-        here = kv == m
-        best, masses, weights, pool_weights = [], [], [], []
-        for r in range(ROWS):
-            top = jnp.max(jnp.where(of_rows[r], tops_in, NEG), axis=1, keepdims=True)
-            top = jnp.maximum(top, jnp.where(here, pool_top[r], NEG))
-            w = jnp.where(of_rows[r], jnp.exp2((tops_in - top) * FACTOR), 0.0)
-            w_pool = jnp.where(here, jnp.exp2((pool_top[r] - top) * FACTOR), 0.0)
-            masses.append(jnp.sum(w * sums_in, axis=1, keepdims=True) + w_pool * pool_sum[r])
-            best.append(top)
-            weights.append(w)
-            pool_weights.append(w_pool)
-        w_1, w_2 = split(jnp.concatenate(weights, axis=0))
-        x = jnp.concatenate([rxc[g, 16 * m : 16 * m + 16, :] for g in range(dp_n)], axis=0)
-        w_1, w_2 = (v[:, : 16 * dp_n].astype(BF16) for v in (w_1, w_2))
-        acc = dot_nn(w_1, x) + dot_nn(w_2, x)
-        accs = [
-            acc[8 * r : 8 * r + 8] + pool_weights[r] * pool_acc[8 * r : 8 * r + 8]
-            for r in range(ROWS)
-        ]
-        def halves(v):
-            low_half, high_half = [], []
-            for pair in range(2):
-                a, b = v[2 * pair], v[2 * pair + 1]
-                low_half.append(jnp.where(sub < 4, a, pltpu.roll(b, 4, 0)))
-                high_half.append(jnp.where(sub < 4, pltpu.roll(a, 4, 0), b))
-            return low_half, high_half
-
-        acc_halves = halves(accs)
-        stat_halves = halves([jnp.where(lane % 64 < 32, best[r], masses[r]) for r in range(ROWS)])
-        for s in range(2):
-            to = 2 * m + s
-            tx2[to, 0:8, :] = acc_halves[s][0]
-            tx2[to, 8:16, :] = acc_halves[s][1]
-            tx2[to, 16:24, :] = jnp.where(lane < 64, stat_halves[s][0], stat_halves[s][1])
-
-    for to in tp_partners:
+        rows = [slice(16 * g + 8 * s, 16 * g + 8 * s + 8) for s in range(2)]
+        tile = share_tile([acc[r] for r in rows], [best[r] for r in rows], [mass[r] for r in rows])
+        tx2[g] = jnp.concatenate(tile, axis=0)
+    for to in dp_partners:
         c2(to).start()
-    rx2[t] = tx2[t]
+    rx2[d] = tx2[d]
 
     new_kv_f[...] = new_kv_v[...].astype(F32)
     keys, values = [], []
@@ -519,12 +494,14 @@
     )
     res = jnp.concatenate([residual_v[:, :side], residual_v[:, side:]], axis=0).astype(F32)
 
-    each_tp(lambda come: c2_from(come).wait_recv())
+    pool_to_mate.wait_recv()
+    each_dp(lambda come: c2_from(come).wait_recv())
+    parts = [shares.at[j] for j in range(2)] + [rx2.at[j] for j in range(dp_n)]
     new_low = jnp.broadcast_to(score_new[0:8], (8, HD))
     new_high = jnp.broadcast_to(score_new[8:16], (8, HD))
     top = jnp.where(lane < 64, new_low, new_high)
-    for j in range(tp_n):
-        top = jnp.maximum(top, rx2[j, 16:24, :])
+    for part in parts:
+        top = jnp.maximum(top, part[16:24, :])
     top = jnp.where(lane % 64 < 32, top, pltpu.roll(top, 32, 1))
     score = jnp.where(lane < 64, new_low, new_high)
     weight = jnp.exp2((score - top) * FACTOR)
@@ -535,12 +512,12 @@
         return jnp.where(lane < 64, v, other), jnp.where(lane < 64, other, v)
 
     acc = [w * value_new[8 * s : 8 * s + 8] for s, w in enumerate(wide_rows(weight))]
-    for j in range(tp_n):
-        their = rx2[j, 16:24, :]
+    for part in parts:
+        their = part[16:24, :]
         w = jnp.exp2((jnp.where(lane % 64 < 32, their, pltpu.roll(their, 32, 1)) - top) * FACTOR)
         mass = mass + w * their
         for s, v in enumerate(wide_rows(w)):
-            acc[s] = acc[s] + v * rx2[j, 8 * s : 8 * s + 8, :]
+            acc[s] = acc[s] + v * part[8 * s : 8 * s + 8, :]
     mass = jnp.where(lane % 64 < 32, pltpu.roll(mass, HD - 32, 1), mass)
     attended = [acc[s] / v for s, v in enumerate(wide_rows(mass))]
 
@@ -602,8 +579,9 @@
     to_mate.wait_send()
     each_dp(lambda to: a1(to).wait_send())
     each_tp(lambda to: a2(to).wait_send())
-    each_dp(lambda to: c1(to).wait_send())
-    each_tp(lambda to: c2(to).wait_send())
+    pool_to_mate.wait_send()
+    each_tp(lambda to: c1(to).wait_send())
+    each_dp(lambda to: c2(to).wait_send())
     each_tp(lambda to: d_copy(to).wait_send())
     each_tp(lambda come: e_from(come).wait_recv())
     square = rx4[0]
@@ -629,14 +607,12 @@
     fresh_rows = fresh_kv.reshape(fresh_n * 2 * kv_n * BLOCK_TOKENS, HD)
     hbm = pl.BlockSpec(memory_space=pltpu.HBM)
     dma = pltpu.SemaphoreType.DMA
-    message = 16 * kv_n + 16
     return pl.pallas_call(
         functools.partial(kernel, dp_n, tp_n, fresh_n, block_n),
         out_shape=jax.ShapeDtypeStruct((ROWS, share), BF16),
         in_specs=[hbm] * 12,
         out_specs=pl.BlockSpec(memory_space=pltpu.VMEM),
         scratch_shapes=[
-            pltpu.SMEM(routes.shape, jnp.int32),
             pltpu.SMEM(block_counts.shape, jnp.int32),
             pltpu.SMEM(tail_fill.shape, jnp.int32),
             pltpu.VMEM(routes.shape, jnp.int32),
@@ -663,26 +639,23 @@
             pltpu.VMEM((fresh_n, head_n, HD), F32),
             pltpu.VMEM((HD, HD), F32),
             pltpu.VMEM((HD, HD), F32),
-            pltpu.VMEM((fresh_n, 8, HD), F32),
-            pltpu.VMEM((fresh_n, 8, HD), F32),
-            pltpu.VMEM((dp_n, message, HD), BF16),
-            pltpu.VMEM((dp_n, message, HD), BF16),
-            pltpu.VMEM((tp_n, 24, HD), F32),
-            pltpu.VMEM((tp_n, 24, HD), F32),
+            pltpu.VMEM((tp_n, 32, HD), BF16),
+            pltpu.VMEM((tp_n, 32, HD), BF16),
+            pltpu.VMEM((24, HD), F32),
+            pltpu.VMEM((2, 24, HD), F32),
+            pltpu.VMEM((dp_n, 24, HD), F32),
+            pltpu.VMEM((dp_n, 24, HD), F32),
             pltpu.VMEM((tp_n, 8, share // 2), F32),
             pltpu.VMEM((tp_n, 8, share // 2), F32),
             pltpu.VMEM((8, HD), F32),
             pltpu.VMEM((tp_n, 8, HD), F32),
-            dma((10,)),
+            dma((9,)),
             dma((block_n // POOL_CHUNK,)),
-            dma(()),
-            dma(()),
-            dma(()),
-            dma(()),
+            *[dma(())] * 6,
             *[dma((dp_n,))] * 2,
-            *[dma((tp_n,))] * 2,
+            *[dma((tp_n,))] * 4,
             *[dma((dp_n,))] * 2,
-            *[dma((tp_n,))] * 6,
+            *[dma((tp_n,))] * 4,
         ],
         compiler_params=pltpu.CompilerParams(
             collective_id=0, has_side_effects=True, vmem_limit_bytes=56 << 20

time: 43.1 us -> 42.1 us (0.977)
  Pallas kernels: 41.7 us -> 40.7 us
    pallas_call x1, Pallas kernels: 41.7 us -> 40.7 us  [local(): pl.pallas_call(functools.partial(kernel, dp_n, tp_n, fresh_n, block_n), o...]
where the time goes in v4:
time: 42.1 us; the launch traced here: 41.9 us
  Pallas kernels  40.7 us (97%)
  local copies, waits for them, and re-layouts  1.28 us (3%)
    pallas_call x1, Pallas kernels, local(): pl.pallas_call(functools.partial(kernel, dp_n, tp_n, fresh_n, block_n), o...  40.7 us
    unnamed x1, local copies, waits for them, and re-layouts  1.28 us

profile of v4, /device:TPU:0, one launch (start us, length us, event | category | flops | bytes accessed | tf_op | source)
XLA Modules:
  0.0 41.9 jit_solution(1577626173370507281)
XLA Ops:
  0.0 40.7 %shard_map.118 = bf16[4,512]{1,0:T(4,128)(2,1)} custom-call(bf16[32768,128]{1,0:T(8,128)(2,1)} %bitcast.4, bf16[12288,128]{1,0:T(8,128)(2,1)} %bitcast.5, bf16[512,8192]{1,0:T(8,128)(2,1)} %w_hbm.1, s32[768]{0:T(1024)} %routes_hbm.1, s32[1,4]{1,0:T(1,128)} %counts_hbm.1, s32[4]{0:T(128)} %tail_hbm.1, s32[1,256]{1,0:T(1,128)} %landing_hbm.1, ...), custom_call_target="tpu_custom_call" | custom-call | tf_op jit(solution)/shard_map/pallas_call | solution.py:610
  40.7 1.3 %copy.14 = bf16[4,512]{1,0:T(4,128)(2,1)} copy(bf16[4,512]{1,0:T(4,128)(2,1)} %shard_map.118) | data formatting | bytes 8192

commit v5 on v4

--- a/solution.py
+++ b/solution.py
@@ -46,7 +46,7 @@
     counts_s, tail_s, routes_v, landing_v, order_v, queries_v, new_kv_v, residual_v, gain_v,
     pool_v, fresh_v, w_v, scores, lim, qf, q_own_v, q_mate, new_kv_f,
     tx0, rx0, picks, rx1, fscore, facc, stat, stat_t,
-    txc, rxc, tx_pool, shares, tx2, rx2, tx3, rx3, tx4, rx4,
+    mixed, keys_v, values_v, txc, rxc, tx_pool, shares, tx2, rx2, tx3, rx3, tx4, rx4,
     small_sem, pool_sem, fresh_sem, w_sem,
     mate_send, mate_recv, pool_send, pool_recv, a1_send, a1_recv, a2_send, a2_recv,
     c1_send, c1_recv, c2_send, c2_recv, d_send, d_recv, e_send, e_recv,
@@ -123,6 +123,7 @@
 
     fresh_copy = pltpu.make_async_copy(fresh_hbm, fresh_v, fresh_sem)
     w_copy = pltpu.make_async_copy(w_hbm, w_v, w_sem)
+    fresh_copy.start()
     loop(0, chunk_n, lambda c: pool_copy(c).start())
 
     sub = iota((8, HD), 0)
@@ -199,7 +200,6 @@
     for to in dp_partners:
         a1(to).start()
     to_mate.start()
-    fresh_copy.start()
     w_copy.start()
     rx0[d] = tx0[d]
 
@@ -225,6 +225,19 @@
     pick_head = pick_head.astype(F32)
     live_row = iota((8 * fresh_n, HD), 0) // 8
     live_from = jnp.where(iota((8 * fresh_n, HD), 1) == t * fresh_n + live_row, 1.0, 0.0).astype(BF16)
+
+    fresh_copy.wait()
+
+    def part_rows(i, carry):
+        piece = fresh_v.shape[0] // fresh_n
+        base = pl.multiple_of(i * piece, piece)
+        mixed[...] = fresh_v[pl.ds(base, piece), :].astype(F32)
+        low_base = pl.multiple_of(i * (piece // 2), piece // 2)
+        keys_v[pl.ds(low_base, piece // 2), :] = mixed[pl.ds(0, piece // 2, stride=2), :].astype(BF16)
+        values_v[pl.ds(low_base, piece // 2), :] = mixed[pl.ds(1, piece // 2, stride=2), :].astype(BF16)
+        return carry
+
+    lax.fori_loop(0, fresh_n, part_rows, 0)
 
     each_dp(lambda come: a1_from(come).wait_recv())
     facts = rx0[0, 16:32, :].astype(F32)[0:8]
@@ -295,13 +308,12 @@
     tops = lax.fori_loop(0, chunk_n, pool_scores, (jnp.full((8, HD), NEG, F32),) * ROWS)
     pool_top = [jnp.maximum(jnp.max(x, axis=1, keepdims=True), 0.1 * NEG) for x in tops]
 
-    fresh_copy.wait()
-    wide = iota((8, 2 * HD), 1)
-    token = jnp.where(wide % 2 == 0, wide // 2, 1 << 20).astype(F32)
+    token = lane.astype(F32)
     each_tp(lambda come: a2_from(come).wait_recv())
 
     def unit(i, k):
-        return (i * kv_n + k) * 2 * BLOCK_TOKENS
+        at = (i * kv_n + k) * BLOCK_TOKENS
+        return slice(at, at + BLOCK_TOKENS)
 
     for k in range(kv_n):
         sides = [rx1[2 * k + s].astype(F32) for s in range(2)]
@@ -312,21 +324,17 @@
             else:
                 a = pltpu.roll(a, 4, 0)
             q_k = jnp.where(sub < 4, a, b).astype(BF16)
-            at = unit(i, k)
-            fscore[(i * kv_n + k) * 8 : (i * kv_n + k) * 8 + 8, :] = dot_nt(
-                q_k, fresh_v[at : at + 2 * BLOCK_TOKENS, :]
-            )
+            at = (i * kv_n + k) * 8
+            fscore[at : at + 8, :] = dot_nt(q_k, keys_v[unit(i, k), :])
     kept = [jnp.zeros((8, HD), F32)] * kv_n
     for i in range(fresh_n):
-        live = live_tokens[8 * i : 8 * i + 8]
-        seen = token < jnp.concatenate([live, live], axis=1)
+        seen = token < live_tokens[8 * i : 8 * i + 8]
         for k in range(kv_n):
             at = (i * kv_n + k) * 8
             s = jnp.where(seen, fscore[at : at + 8, :], NEG)
             top = jnp.max(s, axis=1, keepdims=True)
             p = jnp.exp2((s - top) * FACTOR)
             total = jnp.sum(p, axis=1, keepdims=True)
-            p = jnp.concatenate([pltpu.roll(p[:, :HD], 1, 1), pltpu.roll(p[:, HD:], 1, 1)], axis=1)
             fscore[at : at + 8, :] = p
             kept[k] = jnp.where(lane == i, top, kept[k])
             kept[k] = jnp.where(lane == 8 + i, total, kept[k])
@@ -335,8 +343,7 @@
         for k in range(kv_n):
             at = (i * kv_n + k) * 8
             facc[i, 8 * k : 8 * k + 8, :] = dot_nn(
-                fscore[at : at + 8, :].astype(BF16),
-                fresh_v[unit(i, k) : unit(i, k) + 2 * BLOCK_TOKENS, :],
+                fscore[at : at + 8, :].astype(BF16), values_v[unit(i, k), :]
             )
     stat_t[...] = jnp.transpose(stat[...])
     own_lanes = (lane // OWN == sub) & (sub < fresh_n)
@@ -546,10 +553,12 @@
             last_rows, w_v[:, pl.ds(base + side, side)]
         )
 
-    for at in range(0, tp_n - 1, 5):
-        for to in tp_partners[at : at + 5]:
+    distances = [far(a, tp_side) + far(b, tp_side) for a, b in tp_steps]
+    for distance in sorted(set(distances), reverse=True):
+        equal = [to for to, other in zip(tp_partners, distances) if other == distance]
+        for to in equal:
             tx3[to] = project(to)
-        for to in tp_partners[at : at + 5]:
+        for to in equal:
             d_copy(to).start()
     rx3[t] = res + project(t)
     each_tp(lambda come: d_from(come).wait_recv())
@@ -635,10 +644,13 @@
             pltpu.VMEM((dp_n, 32, HD), BF16),
             pltpu.VMEM((32 * tp_n, HD), BF16),
             pltpu.VMEM((tp_n, 32, HD), BF16),
-            pltpu.VMEM((fresh_n * head_n, 2 * HD), F32),
+            pltpu.VMEM((fresh_n * head_n, HD), F32),
             pltpu.VMEM((fresh_n, head_n, HD), F32),
             pltpu.VMEM((HD, HD), F32),
             pltpu.VMEM((HD, HD), F32),
+            pltpu.VMEM((fresh_rows.shape[0] // fresh_n, HD), F32),
+            pltpu.VMEM((fresh_rows.shape[0] // 2, HD), BF16),
+            pltpu.VMEM((fresh_rows.shape[0] // 2, HD), BF16),
             pltpu.VMEM((tp_n, 32, HD), BF16),
             pltpu.VMEM((tp_n, 32, HD), BF16),
             pltpu.VMEM((24, HD), F32),

time: 42.1 us -> 41 us (0.974)
  Pallas kernels: 40.7 us -> 39.5 us
    pallas_call x1, Pallas kernels: 40.7 us -> 39.5 us  [local(): pl.pallas_call(functools.partial(kernel, dp_n, tp_n, fresh_n, block_n), o...]
where the time goes in v5:
time: 41 us; the launch traced here: 40.8 us
  Pallas kernels  39.5 us (96%)
  local copies, waits for them, and re-layouts  1.28 us (3%)
    pallas_call x1, Pallas kernels, local(): pl.pallas_call(functools.partial(kernel, dp_n, tp_n, fresh_n, block_n), o...  39.5 us
    unnamed x1, local copies, waits for them, and re-layouts  1.28 us

profile of v5, /device:TPU:0, one launch (start us, length us, event | category | flops | bytes accessed | tf_op | source)
XLA Modules:
  0.0 40.8 jit_solution(7904770949147398836)
XLA Ops:
  0.0 39.5 %shard_map.118 = bf16[4,512]{1,0:T(4,128)(2,1)} custom-call(bf16[32768,128]{1,0:T(8,128)(2,1)} %bitcast.4, bf16[12288,128]{1,0:T(8,128)(2,1)} %bitcast.5, bf16[512,8192]{1,0:T(8,128)(2,1)} %w_hbm.1, s32[768]{0:T(1024)} %routes_hbm.1, s32[1,4]{1,0:T(1,128)} %counts_hbm.1, s32[4]{0:T(128)} %tail_hbm.1, s32[1,256]{1,0:T(1,128)} %landing_hbm.1, ...), custom_call_target="tpu_custom_call" | custom-call | tf_op jit(solution)/shard_map/pallas_call | solution.py:619
  39.5 1.3 %copy.14 = bf16[4,512]{1,0:T(4,128)(2,1)} copy(bf16[4,512]{1,0:T(4,128)(2,1)} %shard_map.118) | data formatting | bytes 8192

commit v6 on v5

--- a/solution.py
+++ b/solution.py
@@ -547,6 +547,9 @@
             device_id=(d, come), device_id_type=MESH,
         )
 
+    def pieces(x):
+        return jnp.concatenate([x[:, :HD], x[:, HD:]], axis=0).astype(BF16)
+
     def project(to):
         base = pl.multiple_of(to * share, share)
         return dot_nn(first_rows, w_v[:, pl.ds(base, side)]) + dot_nn(
@@ -557,14 +560,16 @@
     for distance in sorted(set(distances), reverse=True):
         equal = [to for to, other in zip(tp_partners, distances) if other == distance]
         for to in equal:
-            tx3[to] = project(to)
+            tx3[to] = pieces(project(to))
         for to in equal:
             d_copy(to).start()
-    rx3[t] = res + project(t)
+    own = res + project(t)
+    rx3[t] = pieces(jnp.zeros_like(own))
     each_tp(lambda come: d_from(come).wait_recv())
-    hidden = rx3[0]
+    hidden = rx3[0].astype(F32)
     for j in range(1, tp_n):
-        hidden = hidden + rx3[j]
+        hidden = hidden + rx3[j].astype(F32)
+    hidden = own + jnp.concatenate([hidden[0:8], hidden[8:16]], axis=1)
 
     square = jnp.sum(hidden * hidden, axis=1, keepdims=True)
     square = jnp.broadcast_to(square, (8, HD))
@@ -657,8 +662,8 @@
             pltpu.VMEM((2, 24, HD), F32),
             pltpu.VMEM((dp_n, 24, HD), F32),
             pltpu.VMEM((dp_n, 24, HD), F32),
-            pltpu.VMEM((tp_n, 8, share // 2), F32),
-            pltpu.VMEM((tp_n, 8, share // 2), F32),
+            pltpu.VMEM((tp_n, 16, share // 4), BF16),
+            pltpu.VMEM((tp_n, 16, share // 4), BF16),
             pltpu.VMEM((8, HD), F32),
             pltpu.VMEM((tp_n, 8, HD), F32),
             dma((9,)),

time: 41 us -> 40.7 us (level)
  no operation moved by 1% of the time
where the time goes in v6:
time: 40.7 us; the launch traced here: 40.6 us
  Pallas kernels  39.3 us (97%)
  local copies, waits for them, and re-layouts  1.28 us (3%)
    pallas_call x1, Pallas kernels, local(): pl.pallas_call(functools.partial(kernel, dp_n, tp_n, fresh_n, block_n), o...  39.3 us
    unnamed x1, local copies, waits for them, and re-layouts  1.28 us

profile of v6, /device:TPU:0, one launch (start us, length us, event | category | flops | bytes accessed | tf_op | source)
XLA Modules:
  0.0 40.6 jit_solution(12293317346002059173)
XLA Ops:
  0.0 39.3 %shard_map.118 = bf16[4,512]{1,0:T(4,128)(2,1)} custom-call(bf16[32768,128]{1,0:T(8,128)(2,1)} %bitcast.4, bf16[12288,128]{1,0:T(8,128)(2,1)} %bitcast.5, bf16[512,8192]{1,0:T(8,128)(2,1)} %w_hbm.1, s32[768]{0:T(1024)} %routes_hbm.1, s32[1,4]{1,0:T(1,128)} %counts_hbm.1, s32[4]{0:T(128)} %tail_hbm.1, s32[1,256]{1,0:T(1,128)} %landing_hbm.1, ...), custom_call_target="tpu_custom_call" | custom-call | tf_op jit(solution)/shard_map/pallas_call | solution.py:624
  39.3 1.3 %copy.14 = bf16[4,512]{1,0:T(4,128)(2,1)} copy(bf16[4,512]{1,0:T(4,128)(2,1)} %shard_map.118) | data formatting | bytes 8192

commit v7 on v5

--- a/solution.py
+++ b/solution.py
@@ -45,7 +45,7 @@
     out_ref,
     counts_s, tail_s, routes_v, landing_v, order_v, queries_v, new_kv_v, residual_v, gain_v,
     pool_v, fresh_v, w_v, scores, lim, qf, q_own_v, q_mate, new_kv_f,
-    tx0, rx0, picks, rx1, fscore, facc, stat, stat_t,
+    tx0, rx0, picks, rx1, fscore, facc, stat_t,
     mixed, keys_v, values_v, txc, rxc, tx_pool, shares, tx2, rx2, tx3, rx3, tx4, rx4,
     small_sem, pool_sem, fresh_sem, w_sem,
     mate_send, mate_recv, pool_send, pool_recv, a1_send, a1_recv, a2_send, a2_recv,
@@ -309,56 +309,10 @@
     pool_top = [jnp.maximum(jnp.max(x, axis=1, keepdims=True), 0.1 * NEG) for x in tops]
 
     token = lane.astype(F32)
-    each_tp(lambda come: a2_from(come).wait_recv())
+    own_lanes = (lane // OWN == sub) & (sub < fresh_n)
 
     def unit(i, k):
-        at = (i * kv_n + k) * BLOCK_TOKENS
-        return slice(at, at + BLOCK_TOKENS)
-
-    for k in range(kv_n):
-        sides = [rx1[2 * k + s].astype(F32) for s in range(2)]
-        for i in range(fresh_n):
-            a, b = (x[8 * (i // 2) : 8 * (i // 2) + 8] for x in sides)
-            if i % 2 == 0:
-                b = pltpu.roll(b, 4, 0)
-            else:
-                a = pltpu.roll(a, 4, 0)
-            q_k = jnp.where(sub < 4, a, b).astype(BF16)
-            at = (i * kv_n + k) * 8
-            fscore[at : at + 8, :] = dot_nt(q_k, keys_v[unit(i, k), :])
-    kept = [jnp.zeros((8, HD), F32)] * kv_n
-    for i in range(fresh_n):
-        seen = token < live_tokens[8 * i : 8 * i + 8]
-        for k in range(kv_n):
-            at = (i * kv_n + k) * 8
-            s = jnp.where(seen, fscore[at : at + 8, :], NEG)
-            top = jnp.max(s, axis=1, keepdims=True)
-            p = jnp.exp2((s - top) * FACTOR)
-            total = jnp.sum(p, axis=1, keepdims=True)
-            fscore[at : at + 8, :] = p
-            kept[k] = jnp.where(lane == i, top, kept[k])
-            kept[k] = jnp.where(lane == 8 + i, total, kept[k])
-    stat[...] = jnp.concatenate(kept + [jnp.zeros((HD - 8 * kv_n, HD), F32)], axis=0)
-    for i in range(fresh_n):
-        for k in range(kv_n):
-            at = (i * kv_n + k) * 8
-            facc[i, 8 * k : 8 * k + 8, :] = dot_nn(
-                fscore[at : at + 8, :].astype(BF16), values_v[unit(i, k), :]
-            )
-    stat_t[...] = jnp.transpose(stat[...])
-    own_lanes = (lane // OWN == sub) & (sub < fresh_n)
-
-    def shifted(x):
-        return jnp.concatenate(
-            [pltpu.roll(x[i : i + 1], OWN * i, 1) if i else x[0:1] for i in range(8)], axis=0
-        )
-
-    tops_of, sums_of = shifted(stat_t[0:8, :]), shifted(stat_t[8:16, :])
-
-    def row_for(x, to):
-        x = pltpu.roll(x, HD - OWN * to, 1) if to else x
-        x = jnp.sum(jnp.where(own_lanes, x, 0.0), axis=0, keepdims=True)
-        return jnp.broadcast_to(x, (8, HD))
+        return pl.ds(pl.multiple_of((i * kv_n + k) * BLOCK_TOKENS, BLOCK_TOKENS), BLOCK_TOKENS)
 
     def halves(v):
         low_half, high_half = [], []
@@ -367,19 +321,15 @@
             high_half.append(jnp.where(sub < 4, pltpu.roll(a, 4, 0), b))
         return low_half, high_half
 
-    for k in range(kv_n):
-        tiles_of = halves([facc[i, 8 * k : 8 * k + 8, :] for i in range(fresh_n)])
-        for s in range(2):
-            to = 2 * k + s
-            top_1, rest = split(row_for(tops_of, to))
-            top_2, top_3 = split(rest)
-            sum_1, sum_2 = split(row_for(sums_of, to))
-            x = jnp.where(sub == 0, top_1, jnp.where(sub == 1, top_2, top_3))
-            x = jnp.where(sub < 3, x, jnp.where(sub == 3, sum_1, sum_2))
-            x = jnp.where((sub < 5) & (lane < fresh_n * OWN), x, 0.0)
-            x = pltpu.roll(x, lax.rem(t, 4) * 32, 1)
-            gap = [jnp.zeros((8, HD), F32)] * (3 - len(tiles_of[s]))
-            txc[to] = jnp.concatenate(tiles_of[s] + gap + [x], axis=0).astype(BF16)
+    def shifted(x):
+        return jnp.concatenate(
+            [pltpu.roll(x[i : i + 1], OWN * i, 1) if i else x[0:1] for i in range(8)], axis=0
+        )
+
+    def row_for(x, spot_at):
+        x = pltpu.roll(x, HD - OWN * spot_at, 1) if spot_at else x
+        x = jnp.sum(jnp.where(own_lanes, x, 0.0), axis=0, keepdims=True)
+        return jnp.broadcast_to(x, (8, HD))
 
     def c1(to):
         return pltpu.make_async_remote_copy(
@@ -393,8 +343,65 @@
             device_id=(d, come), device_id_type=MESH,
         )
 
-    for to in tp_partners:
-        c1(to).start()
+    def fresh_heads(heads):
+        for p, k in enumerate(heads):
+            sides = [rx1[2 * k + s].astype(F32) for s in range(2)]
+            for i in range(fresh_n):
+                a, b = (x[8 * (i // 2) : 8 * (i // 2) + 8] for x in sides)
+                if i % 2 == 0:
+                    b = pltpu.roll(b, 4, 0)
+                else:
+                    a = pltpu.roll(a, 4, 0)
+                q_k = jnp.where(sub < 4, a, b).astype(BF16)
+                at = (i * kv_n + p) * 8
+                fscore[at : at + 8, :] = dot_nt(q_k, keys_v[unit(i, k), :])
+        kept = [jnp.zeros((8, HD), F32)] * len(heads)
+        for i in range(fresh_n):
+            seen = token < live_tokens[8 * i : 8 * i + 8]
+            for p in range(len(heads)):
+                at = (i * kv_n + p) * 8
+                s = jnp.where(seen, fscore[at : at + 8, :], NEG)
+                top = jnp.max(s, axis=1, keepdims=True)
+                w = jnp.exp2((s - top) * FACTOR)
+                total = jnp.sum(w, axis=1, keepdims=True)
+                fscore[at : at + 8, :] = w
+                kept[p] = jnp.where(lane == i, top, kept[p])
+                kept[p] = jnp.where(lane == 8 + i, total, kept[p])
+        rest_rows = jnp.zeros((HD - 8 * len(heads), HD), F32)
+        stat_t[...] = jnp.transpose(jnp.concatenate(kept + [rest_rows], axis=0))
+        for i in range(fresh_n):
+            for p, k in enumerate(heads):
+                at = (i * kv_n + p) * 8
+                facc[i, 8 * p : 8 * p + 8, :] = dot_nn(
+                    fscore[at : at + 8, :].astype(BF16), values_v[unit(i, k), :]
+                )
+        tops_of, sums_of = shifted(stat_t[0:8, :]), shifted(stat_t[8:16, :])
+        for p, k in enumerate(heads):
+            tiles_of = halves([facc[i, 8 * p : 8 * p + 8, :] for i in range(fresh_n)])
+            for s in range(2):
+                top_1, rest = split(row_for(tops_of, 2 * p + s))
+                top_2, top_3 = split(rest)
+                sum_1, sum_2 = split(row_for(sums_of, 2 * p + s))
+                x = jnp.where(sub == 0, top_1, jnp.where(sub == 1, top_2, top_3))
+                x = jnp.where(sub < 3, x, jnp.where(sub == 3, sum_1, sum_2))
+                x = jnp.where((sub < 5) & (lane < fresh_n * OWN), x, 0.0)
+                x = pltpu.roll(x, lax.rem(t, 4) * 32, 1)
+                gap = [jnp.zeros((8, HD), F32)] * (3 - len(tiles_of[s]))
+                txc[2 * k + s] = jnp.concatenate(tiles_of[s] + gap + [x], axis=0).astype(BF16)
+
+    line_heads = tp_side // 2
+    for distance in range(tp_side // 2 + 1):
+        lines = [dx for dx in range(tp_side) if far(dx, tp_side) == distance]
+        partners = [to for to, (dx, _) in zip(tp_partners, tp_steps) if dx in lines]
+        for come in reversed(partners):
+            a2_from(come).wait_recv()
+        heads = []
+        for dx in lines:
+            line = lax.rem(t // tp_side + dx, tp_side)
+            heads += [line * line_heads + n for n in range(line_heads)]
+        fresh_heads(heads)
+        for to in partners:
+            c1(to).start()
     rxc[t] = txc[t]
 
     def pool_values(c, carry):
@@ -647,7 +654,6 @@
             pltpu.VMEM((fresh_n * head_n, HD), F32),
             pltpu.VMEM((fresh_n, head_n, HD), F32),
             pltpu.VMEM((HD, HD), F32),
-            pltpu.VMEM((HD, HD), F32),
             pltpu.VMEM((fresh_rows.shape[0] // fresh_n, HD), F32),
             pltpu.VMEM((fresh_rows.shape[0] // 2, HD), BF16),
             pltpu.VMEM((fresh_rows.shape[0] // 2, HD), BF16),

time: 41 us -> 40.8 us (level)
  no operation moved by 1% of the time
where the time goes in v7:
time: 40.8 us; the launch traced here: 40.7 us
  Pallas kernels  39.4 us (97%)
  local copies, waits for them, and re-layouts  1.28 us (3%)
    pallas_call x1, Pallas kernels, local(): pl.pallas_call(functools.partial(kernel, dp_n, tp_n, fresh_n, block_n), o...  39.4 us
    unnamed x1, local copies, waits for them, and re-layouts  1.28 us

profile of v7, /device:TPU:0, one launch (start us, length us, event | category | flops | bytes accessed | tf_op | source)
XLA Modules:
  0.0 40.7 jit_solution(10657813728252514723)
XLA Ops:
  0.0 39.4 %shard_map.118 = bf16[4,512]{1,0:T(4,128)(2,1)} custom-call(bf16[32768,128]{1,0:T(8,128)(2,1)} %bitcast.4, bf16[12288,128]{1,0:T(8,128)(2,1)} %bitcast.5, bf16[512,8192]{1,0:T(8,128)(2,1)} %w_hbm.1, s32[768]{0:T(1024)} %routes_hbm.1, s32[1,4]{1,0:T(1,128)} %counts_hbm.1, s32[4]{0:T(128)} %tail_hbm.1, s32[1,256]{1,0:T(1,128)} %landing_hbm.1, ...), custom_call_target="tpu_custom_call" | custom-call | tf_op jit(solution)/shard_map/pallas_call | solution.py:626
  39.4 1.3 %copy.14 = bf16[4,512]{1,0:T(4,128)(2,1)} copy(bf16[4,512]{1,0:T(4,128)(2,1)} %shard_map.118) | data formatting | bytes 8192

commit v8 on v7

--- a/solution.py
+++ b/solution.py
@@ -574,24 +574,24 @@
         hidden = hidden + rx3[j]
 
     square = jnp.sum(hidden * hidden, axis=1, keepdims=True)
-    square = jnp.broadcast_to(square, (8, HD))
-    tx4[...] = square + pltpu.roll(square, 4, 0)
+    square = jnp.where(lane % ROWS == sub % ROWS, jnp.broadcast_to(square, (8, HD)), 0.0)
+    tx4[0:1, :] = jnp.sum(square, axis=0, keepdims=True)
 
     def e_copy(to):
         return pltpu.make_async_remote_copy(
-            tx4, rx4.at[t], e_send.at[to], e_recv.at[t],
+            tx4.at[pl.ds(0, 1)], rx4.at[t, pl.ds(0, 1)], e_send.at[to], e_recv.at[t],
             device_id=(d, to), device_id_type=MESH,
         )
 
     def e_from(come):
         return pltpu.make_async_remote_copy(
-            tx4, rx4.at[come], e_send.at[come], e_recv.at[come],
+            tx4.at[pl.ds(0, 1)], rx4.at[come, pl.ds(0, 1)], e_send.at[come], e_recv.at[come],
             device_id=(d, come), device_id_type=MESH,
         )
 
     for to in tp_partners:
         e_copy(to).start()
-    rx4[t] = tx4[...]
+    rx4[t, 0:1, :] = tx4[0:1, :]
     to_mate.wait_send()
     each_dp(lambda to: a1(to).wait_send())
     each_tp(lambda to: a2(to).wait_send())
@@ -600,9 +600,11 @@
     each_dp(lambda to: c2(to).wait_send())
     each_tp(lambda to: d_copy(to).wait_send())
     each_tp(lambda come: e_from(come).wait_recv())
-    square = rx4[0]
+    square = rx4[0, 0:1, :]
     for j in range(1, tp_n):
-        square = square + rx4[j]
+        square = square + rx4[j, 0:1, :]
+    square = jnp.where(lane == sub % ROWS, jnp.broadcast_to(square, (8, HD)), 0.0)
+    square = jnp.broadcast_to(jnp.sum(square, axis=1, keepdims=True), (8, HD))
     scale = lax.rsqrt(square * (1.0 / width) + 1e-5)
     normed = hidden * jnp.concatenate([scale] * (side // HD), axis=1) * gains
     out_ref[...] = jnp.concatenate([normed[0:ROWS], normed[ROWS:]], axis=1).astype(BF16)

time: 40.8 us -> 40.7 us (level)
  no operation moved by 1% of the time
where the time goes in v8:
time: 40.7 us; the launch traced here: 40.5 us
  Pallas kernels  39.2 us (96%)
  local copies, waits for them, and re-layouts  1.28 us (3%)
    pallas_call x1, Pallas kernels, local(): pl.pallas_call(functools.partial(kernel, dp_n, tp_n, fresh_n, block_n), o...  39.2 us
    unnamed x1, local copies, waits for them, and re-layouts  1.28 us

profile of v8, /device:TPU:0, one launch (start us, length us, event | category | flops | bytes accessed | tf_op | source)
XLA Modules:
  0.0 40.5 jit_solution(17660714428422996248)
XLA Ops:
  0.0 39.2 %shard_map.118 = bf16[4,512]{1,0:T(4,128)(2,1)} custom-call(bf16[32768,128]{1,0:T(8,128)(2,1)} %bitcast.4, bf16[12288,128]{1,0:T(8,128)(2,1)} %bitcast.5, bf16[512,8192]{1,0:T(8,128)(2,1)} %w_hbm.1, s32[768]{0:T(1024)} %routes_hbm.1, s32[1,4]{1,0:T(1,128)} %counts_hbm.1, s32[4]{0:T(128)} %tail_hbm.1, s32[1,256]{1,0:T(1,128)} %landing_hbm.1, ...), custom_call_target="tpu_custom_call" | custom-call | tf_op jit(solution)/shard_map/pallas_call | solution.py:628
  39.2 1.3 %copy.14 = bf16[4,512]{1,0:T(4,128)(2,1)} copy(bf16[4,512]{1,0:T(4,128)(2,1)} %shard_map.118) | data formatting | bytes 8192
